TPU v7x, 32 devices: a whole 2x2x4 slice. The times are simulated.
32 devices in a mesh: groups: 2 (over x), row: 4 (over y, core), col: 4 (over z).
Axes of the slice: x: 2, y: 2, z: 4, core: 2. Of those that a mesh axis runs over, the one named last changes fastest.
Arguments:
- tokens: bfloat16 [1024, 8192], P(('groups', 'row'), 'col'), parts along dimension 0, may hold values from -6 to 6
- gate_weight: bfloat16 [8192, 16384], P('col', 'row'), may hold values from -0.09375 to 0.09375
- up_weight: bfloat16 [8192, 16384], P('col', 'row'), may hold values from -0.09375 to 0.09375
- down_weight: bfloat16 [16384, 8192], P('row', 'col'), may hold values from -0.09375 to 0.09375
- gate_mask: int32 [64, 128], P('col', 'row'), may hold values from 0 to 1, as said below
- up_mask: int32 [64, 128], P('col', 'row'), may hold values from 0 to 1, as said below
- down_mask: int32 [128, 64], P('row', 'col'), may hold values from 0 to 1, as said below
Outputs:
- mixed: bfloat16 [1024, 8192], P(('groups', 'row'), 'col'), parts along dimension 0
There are 2 independent parts, one for each index of `groups`. A program takes and returns all parts, laid end to end along the dimension named above; an argument that names none is the same for every part. Nothing has to cross between parts.
Inputs may be any that keep to these rules, and one draw needn't show every extreme that they name: `gate_mask`: 1 where a 128 x 128 tile of the gate projection is kept, else 0; the share kept differs from one block of 128 hidden units to another. `up_mask`: 1 where a tile of the up projection is kept, else 0. `down_mask`: 1 where a tile of the down projection is kept, else 0.
All inputs are finite; a program needn't handle non-finite values.
Results may differ from a plain program's by a relative error of at most 0.02.
Values may be sent and summed in bfloat16 or wider, within the bound.
No kernel may reach another device: no remote copies, remote signals or barrier semaphores. Data moves between devices by JAX's collectives and lax.ppermute only.
A program may use at most 256 MiB of HBM per device.

v0:
```python
import functools

import jax
import jax.numpy as jnp
from jax import lax
from jax.experimental import pallas as pl
from jax.experimental.pallas import tpu as pltpu
from jax.sharding import PartitionSpec as P

ANY = pl.BlockSpec(memory_space=pl.ANY)
SMEM = pl.BlockSpec(memory_space=pltpu.SMEM)
VMEM = pl.BlockSpec(memory_space=pltpu.VMEM)
MIB = 1 << 20
TOKEN = jax.ShapeDtypeStruct((8, 128), jnp.float32)
BRIEF = pl.CostEstimate(flops=1 << 18, bytes_accessed=1 << 20, transcendentals=0)
LONG = pl.CostEstimate(flops=6 << 30, bytes_accessed=16 << 20, transcendentals=0)


def masked(block, kept, edge):
    strips = []
    for i in range(block.shape[0] // edge):
        tiles = []
        for j in range(block.shape[1] // edge):
            keep = kept(i, j).astype(jnp.float32).astype(jnp.bfloat16)
            tiles.append(block[i * edge:(i + 1) * edge, j * edge:(j + 1) * edge] * keep)
        strips.append(jnp.concatenate(tiles, axis=1))
    return jnp.concatenate(strips, axis=0)


def partial_kernel(edge, unit, first, hand_on, gm_hbm, um_hbm, gate, up, *rest):
    rest, (w, masks, sems, mask_sems) = rest[:-4], rest[-4:]
    *rest, tok_out = rest
    if hand_on:
        *rest, passed = rest
        passed[...] = rest[-3][...]
    *xs, pa, pb = rest if first else rest[1:]
    units = w.shape[2]
    starts = (unit * units, gate.shape[1] // 2 + unit * units)

    def mask_load(plane, src):
        return pltpu.make_async_copy(src, masks.at[plane], mask_sems.at[plane])

    def load(src, side, plane):
        slot = side * 2 + plane
        return pltpu.make_async_copy(src.at[:, pl.ds(starts[side], units)], w.at[slot], sems.at[slot])

    for plane, src in enumerate((gm_hbm, um_hbm)):
        mask_load(plane, src).start()
    for side in range(2):
        for plane, src in enumerate((gate, up)):
            load(src, side, plane).start()
    for plane, src in enumerate((gm_hbm, um_hbm)):
        mask_load(plane, src).wait()
    x = xs[0][...] if len(xs) == 1 else jnp.concatenate([part[...] for part in xs], axis=0)
    part = min(256, units)
    parts = units // part
    for side, out in enumerate((pa, pb)):
        def one(i, _, side=side, out=out):
            plane, n = i // parts, i % parts

            if isinstance(i, int):
                if n == 0:
                    load(gate, side, plane).wait()
                at = pl.ds(n * part, part)
            else:
                @pl.when(n == 0)
                def _():
                    load(gate, side, plane).wait()

                at = pl.ds(pl.multiple_of(n * part, part), part)
            col = starts[side] // edge + n * (part // edge)
            out[plane, :, at] = jnp.dot(
                x, masked(w[side * 2 + plane, :, at], lambda a, b: masks[plane, a, col + b], edge),
                preferred_element_type=jnp.float32,
            ).astype(out.dtype)
            return 0

        if len(xs) > 1:
            for i in range(2 * parts):
                one(i, 0)
        else:
            lax.fori_loop(0, 2 * parts, one, 0)


def partials(tok, xs, gate, up, gm, um, unit, units, hand_on=False):
    rows, depth = xs[0].shape
    out = jax.ShapeDtypeStruct((2, rows * len(xs), units), jnp.bfloat16)
    first = tok is None
    return pl.pallas_call(
        functools.partial(partial_kernel, depth // gm.shape[0], unit, first, hand_on),
        in_specs=[ANY] * (4 if first else 5) + [VMEM] * len(xs),
        out_specs=[VMEM] * (3 if hand_on else 2) + [ANY],
        out_shape=[out, out] + [jax.ShapeDtypeStruct((rows, depth), jnp.bfloat16)] * hand_on + [TOKEN],
        scratch_shapes=[
            pltpu.VMEM((4, depth, units), jnp.bfloat16),
            pltpu.SMEM((2, *gm.shape), jnp.int32),
            pltpu.SemaphoreType.DMA((4,)),
            pltpu.SemaphoreType.DMA((2,)),
        ],
        input_output_aliases={} if first else {4: 3 if hand_on else 2},
        cost_estimate=LONG,
        compiler_params=pltpu.CompilerParams(vmem_limit_bytes=48 * MIB),
    )(gm, um, gate, up, *([] if first else [tok]), *xs)


def swiglu(gate, up):
    return gate / (1.0 + jnp.exp(-gate)) * up


def over(rows, body):
    piece = min(16, rows)

    def one(i, _):
        body(pl.ds(pl.multiple_of(i * piece, piece), piece))
        return 0

    lax.fori_loop(0, rows // piece, one, 0)


def sum_kernel(own, n_col, goes_on, ends, z_ref, tok, left_in, right_in, *rest):
    n_own = len(own[0]) + len(own[1])
    mine, (*outs, tok_out, a, b, sems) = rest[:n_own], rest[n_own:]
    left_out, right_out = outs[:2] if goes_on else (None, None)
    z = z_ref[0]
    rows = a.shape[1]

    def each(act):
        for ref, (i, row), to, sem in zip(
            mine, own[0] + own[1], [a] * len(own[0]) + [b] * len(own[1]), [0] * len(own[0]) + [1] * len(own[1])
        ):
            @pl.when(z == i)
            def _(ref=ref, row=row, to=to, sem=sem):
                act(pltpu.make_async_copy(ref.at[:, pl.ds(row, rows), :], to, sems.at[sem]))

    each(lambda c: c.start())
    each(lambda c: c.wait())
    for side, came, here, goes, origin, end in (
        (0, left_in, a, left_out, n_col - 1, 0), (1, right_in, b, right_out, 0, n_col - 1)
    ):
        if goes_on:
            @pl.when(z == origin)
            def _(here=here, goes=goes):
                goes[...] = here[...]

            @pl.when((z != origin) & (z != end))
            def _(came=came, here=here, goes=goes):
                def add_up(r):
                    for p in range(2):
                        goes[p, r, :] = (came[p, r, :].astype(jnp.float32) + here[p, r, :].astype(jnp.float32)).astype(goes.dtype)
                over(rows, add_up)
        if ends:
            @pl.when(z == end)
            def _(side=side, came=came, here=here):
                def finish(r):
                    gate, up = (came[p, r, :].astype(jnp.float32) + here[p, r, :].astype(jnp.float32) for p in range(2))
                    outs[-1][side, r, :] = swiglu(gate, up).astype(outs[-1].dtype)
                over(rows, finish)


def sum_step(tok, z, left_in, right_in, own_a, own_b, goes_on, ends, n_col):
    _, rows, units = left_in.shape
    out = jax.ShapeDtypeStruct((2, rows, units), jnp.bfloat16)
    outs = [out] * (2 * goes_on + ends)
    own = (tuple(o[:2] for o in own_a), tuple(o[:2] for o in own_b))
    res = pl.pallas_call(
        functools.partial(sum_kernel, own, n_col, goes_on, ends),
        in_specs=[SMEM, ANY, VMEM, VMEM] + [ANY] * (len(own_a) + len(own_b)),
        out_specs=[VMEM] * len(outs) + [ANY],
        out_shape=outs + [TOKEN],
        scratch_shapes=[
            pltpu.VMEM((2, rows, units), jnp.bfloat16),
            pltpu.VMEM((2, rows, units), jnp.bfloat16),
            pltpu.SemaphoreType.DMA((2,)),
        ],
        input_output_aliases={1: len(outs)},
        cost_estimate=BRIEF,
        compiler_params=pltpu.CompilerParams(vmem_limit_bytes=8 * MIB),
    )(z, tok, left_in, right_in, *[o[2] for o in own_a], *[o[2] for o in own_b])
    sums = res[:2] if goes_on else (None, None)
    return sums, res[-2] if ends else None, res[-1]


def relay_kernel(n_col, made, got, z_ref, tok, *rest):
    fresh, rest = (rest[0], rest[1:]) if made else (None, rest)
    came, (left_out, right_out, tok_out) = rest[:-3], rest[-3:]
    z = z_ref[0]
    for side, out, end in ((0, right_out, 0), (1, left_out, n_col - 1)):
        if made:
            @pl.when(z == end)
            def _(side=side, out=out):
                out[...] = fresh[side]
        if got:
            @pl.when(z != end)
            def _(side=side, out=out):
                out[...] = came[side][...]


def relay(tok, z, fresh, came, n_col):
    like = came[0] if came else fresh
    out = jax.ShapeDtypeStruct(like.shape[-2:], jnp.bfloat16)
    made = fresh is not None
    return pl.pallas_call(
        functools.partial(relay_kernel, n_col, made, len(came) > 0),
        in_specs=[SMEM, ANY] + [VMEM] * (made + len(came)),
        out_specs=[VMEM, VMEM, ANY],
        out_shape=[out, out, TOKEN],
        input_output_aliases={1: 2},
        cost_estimate=LONG,
        compiler_params=pltpu.CompilerParams(vmem_limit_bytes=8 * MIB),
    )(z, tok, *([fresh] if made else []), *came)


def project_kernel(picks, edge, first, n_unit, blocks, more, last, unroll, z_ref, mask, tok, down, *rest):
    hidden, rest = rest[:len(picks)], rest[len(picks):]
    if more:
        total, rest = rest[0], rest[1:]
    outs, (tok_out, held, w, sems, w_sems) = rest[:-5], rest[-5:]
    z = z_ref[0]
    units = w.shape[1]
    count = held.shape[0] // 2
    rows = held.shape[1] // blocks
    slabs = 2
    wide = down.shape[1] // slabs
    thin = wide // 2

    def load(j, u, side):
        row = (side * n_unit + first + u) * units
        at = pl.ds(j * wide, wide)
        slot = side * count + u
        return pltpu.make_async_copy(
            down.at[pl.ds(row, units), at], w.at[slot, :, at], w_sems.at[j * (2 * count) + slot]
        )

    def every(act, j):
        for u in range(count):
            for side in range(2):
                act(load(j, u, side))

    for j in range(slabs):
        every(lambda c: c.start(), j)

    def each(act):
        for ref, (i, slot, block) in zip(hidden, picks):
            @pl.when(z == i)
            def _(ref=ref, slot=slot, block=block):
                act(pltpu.make_async_copy(
                    ref, held.at[slot, pl.ds(block * rows, rows), :], sems.at[slot * blocks + block]
                ))

    each(lambda c: c.start())
    each(lambda c: c.wait())

    def one(i, _):
        if unroll:
            if i % 2 == 0:
                every(lambda c: c.wait(), i // 2)
            at = pl.ds(i * thin, thin)
        else:
            for j in range(slabs):
                @pl.when(i == 2 * j)
                def _(j=j):
                    every(lambda c: c.wait(), j)

            at = pl.ds(pl.multiple_of(i * thin, thin), thin)
        terms = None
        for u in range(count):
            for side in range(2):
                slot = side * count + u
                row = (side * n_unit + first + u) * (units // edge)
                kept = masked(w[slot, :, at], lambda a, b: mask[row + a, i * (thin // edge) + b], edge)
                term = jnp.dot(held[slot], kept, preferred_element_type=jnp.float32)
                terms = term if terms is None else terms + term
        if more:
            terms = terms + total[:, at]
        if last:
            for k, out in enumerate(outs):
                out[:, at] = terms[k * rows:(k + 1) * rows, :].astype(out.dtype)
        else:
            outs[0][:, at] = terms
        return 0

    if unroll:
        for i in range(2 * slabs):
            one(i, 0)
    else:
        lax.fori_loop(0, 2 * slabs, one, 0)


def project(tok, z, hidden, down, mask, units, first, count, blocks, total, last, unroll):
    rows = hidden[0][3].shape[0]
    depth, width = down.shape
    edge = depth // mask.shape[0]
    n_unit = depth // 2 // units
    if last:
        out_shape = [jax.ShapeDtypeStruct((rows, width), jnp.bfloat16)] * blocks
    else:
        out_shape = [jax.ShapeDtypeStruct((blocks * rows, width), jnp.float32)]
    more = total is not None
    aliases = {2: len(out_shape)}
    if more and not last:
        aliases[4 + len(hidden)] = 0
    res = pl.pallas_call(
        functools.partial(project_kernel, tuple(h[:3] for h in hidden), edge, first, n_unit, blocks, more, last, unroll),
        in_specs=[SMEM, SMEM, ANY, pl.BlockSpec(memory_space=pltpu.HBM)] + [ANY] * len(hidden) + [VMEM] * more,
        out_specs=[VMEM] * len(out_shape) + [ANY],
        out_shape=out_shape + [TOKEN],
        scratch_shapes=[
            pltpu.VMEM((2 * count, blocks * rows, units), jnp.bfloat16),
            pltpu.VMEM((2 * count, units, width), jnp.bfloat16),
            pltpu.SemaphoreType.DMA((2 * count * blocks,)),
            pltpu.SemaphoreType.DMA((4 * count,)),
        ],
        input_output_aliases=aliases,
        cost_estimate=LONG,
        compiler_params=pltpu.CompilerParams(vmem_limit_bytes=48 * MIB),
    )(z, mask, tok, down, *[h[3] for h in hidden], *([total] if more else []))
    return res[:-1], res[-1]


def add_kernel(tok, x, y, out, tok_out):
    out[...] = (x[...].astype(jnp.float32) + y[...].astype(jnp.float32)).astype(out.dtype)


def add(tok, x, y):
    return pl.pallas_call(
        add_kernel,
        in_specs=[ANY, VMEM, VMEM],
        out_specs=[VMEM, ANY],
        out_shape=[jax.ShapeDtypeStruct(x.shape, x.dtype), TOKEN],
        input_output_aliases={0: 1},
        cost_estimate=BRIEF,
        compiler_params=pltpu.CompilerParams(vmem_limit_bytes=8 * MIB),
    )(tok, x, y)


def cycle(n_row, n_col):
    def at(r, i):
        return r * n_col + (n_col - 1 - i if r % 2 else i)

    steps = []
    for r in range(n_row):
        steps += [(at(r, i), at(r, i + 1)) for i in range(n_col - 1)] + [(at(r, n_col - 1), at(r ^ 1, 0))]
    return steps


def other(i, d, n_row):
    return (i // 2 + d // 2) % (n_row // 2) * 2 + (i % 2 ^ d % 2)


def pieces(group, n_unit):
    count = 2 if n_unit % 2 == 0 else 1
    return [(u, count) for u in range(0, n_unit, count)]


def shards(n_row, n_col, tokens, gate, up, down, gm, um, dm):
    half = gate.shape[1] // 2
    units = min(512, half)
    n_unit = half // units
    rows = tokens.shape[0]
    z, odd = lax.axis_index("col"), lax.axis_index("row") % 2
    z = jnp.where(odd == 1, n_col - 1 - z, z).astype(jnp.int32).reshape(1)
    to_right = cycle(n_row, n_col)
    to_left = [(j, i) for i, j in to_right]
    tok = None

    def swap(x, d, back=False):
        pairs = [(other(i, d, n_row), i) for i in range(n_row)]
        return lax.ppermute(x, "row", [(j, i) for i, j in pairs] if back else pairs)

    groups = [[0]] + [[d, d + 1] for d in range(2, n_row, 2)] + [[1]]
    xs = {0: tokens}
    chunks = [(d, u) for g in groups for u in range(n_unit) for d in g]
    n = len(chunks)
    first_end, last_end = n_col - 1, n + n_col - 2
    last_hop = last_end + n_col - 2
    own_a, own_b = {}, {}
    left_got, right_got, left_on, right_on, left_came, right_came = {}, {}, {}, {}, {}, {}

    def places(k):
        spots = []
        for i in range(n_col):
            t = k + first_end + i
            for side, at, on, came in ((0, i, right_on, right_came), (1, n_col - 1 - i, left_on, left_came)):
                spots.append((at, side, on[t] if t <= last_hop else came[t - 1]))
        return spots

    def compute(group, u):
        def run(tok):
            hand_on = group == [0] and u == min(1, n_unit - 1)
            pa, pb, *passed, tok = partials(tok, [xs[d] for d in group], gate, up, gm, um, u, units, hand_on)
            if hand_on:
                for d in [*range(2, n_row), 1]:
                    xs[d] = swap(passed[0], d)
            for i, d in enumerate(group):
                k = chunks.index((d, u))
                own_a[k], own_b[k] = (i * rows, pa), (i * rows, pb)
            return tok
        return run

    totals, outs, pairs = {}, {}, []

    def down_projection(g, first, count):
        def run(tok):
            hidden = []
            for b, d in enumerate(g):
                for u in range(first, first + count):
                    for i, side, buf in places(chunks.index((d, u))):
                        hidden.append((i, side * count + u - first, b, buf))
            key, last = tuple(g), first + count == n_unit
            res, tok = project(tok, z, hidden, down, dm, units, first, count, len(g), totals.get(key), last, g == [1])
            if last:
                outs.update(zip(g, res))
                if len(g) > 1:
                    pairs.append((g[0], swap(outs.pop(g[1]), 1)))
            else:
                totals[key] = res[0]
            return tok
        return run

    def add_pairs(tok):
        while pairs:
            d, theirs = pairs.pop()
            total, tok = add(tok, outs[d], theirs)
            outs[d] = swap(total, d, back=True)
        return tok

    work = {}
    for g in groups:
        for first, count in pieces(g, n_unit):
            k = max(chunks.index((d, u)) for d in g for u in range(first, first + count))
            work.setdefault(k + 2 * first_end, []).append(down_projection(g, first, count))
    needs = sorted((min(chunks.index((d, u)) for d in g), u, g) for g in groups for u in range(n_unit))
    for k, u, g in reversed(needs):
        at = next((s for s in range(k - 1, -1, -1) if s not in work), k - 1)
        work.setdefault(at, []).insert(0, compute(g, u))

    for run in work.get(-1, []):
        tok = run(tok)
    for t in range(last_hop + 2):
        fresh = None
        if t <= last_end:
            if t == 0:
                sums = own_a[0][1], own_b[0][1]
            else:
                mine_a = [(i, *own_a[t - (n_col - 1 - i)]) for i in range(n_col) if 0 <= t - (n_col - 1 - i) < n]
                mine_b = [(i, *own_b[t - i]) for i in range(n_col) if 0 <= t - i < n]
                sums, fresh, tok = sum_step(
                    tok, z, left_got[t - 1], right_got[t - 1], mine_a, mine_b, t < last_end, t >= first_end, n_col
                )
            if t < last_end:
                left_got[t] = lax.ppermute(sums[0], ("row", "col"), to_left)
                right_got[t] = lax.ppermute(sums[1], ("row", "col"), to_right)
        if first_end <= t <= last_hop:
            came = (right_came[t - 1], left_came[t - 1]) if t > first_end else ()
            left_on[t], right_on[t], tok = relay(tok, z, fresh, came, n_col)
            left_came[t] = lax.ppermute(left_on[t], ("row", "col"), to_left)
            right_came[t] = lax.ppermute(right_on[t], ("row", "col"), to_right)
        tok = add_pairs(tok)
        for run in work.get(t, []):
            tok = run(tok)
    tok = add_pairs(tok)

    mixed = sum(x.astype(jnp.float32) for d, x in outs.items() if d != 1)
    mixed = mixed + swap(outs[1], 1).astype(jnp.float32)
    return mixed.astype(jnp.bfloat16)


def solution(mesh):
    in_specs = (
        P(("groups", "row"), "col"),
        P("col", "row"),
        P("col", "row"),
        P("row", "col"),
        P("col", "row"),
        P("col", "row"),
        P("row", "col"),
    )
    out_specs = P(("groups", "row"), "col")
    body = functools.partial(shards, mesh.shape["row"], mesh.shape["col"])
    return jax.shard_map(body, mesh=mesh, in_specs=in_specs, out_specs=out_specs, check_vma=False)
```

profile of v0, /device:TPU:0, one launch (start us, length us, event | category | flops | bytes accessed | tf_op | source)
XLA Modules:
  0.0 212.2 jit_solution(3672186042890038827)
XLA Ops:
  2.4 4.5 %shard_map.73 = (bf16[2,128,512]{2,1,0:T(8,128)(2,1)S(1)}, bf16[2,128,512]{2,1,0:T(8,128)(2,1)S(1)}, f32[8,128]{1,0:T(8,128)S(1)}) custom-call(s32[16,32]{1,0:T(8,128)S(1)} %copy-done.4, s32[16,32]{1,0:T(8,128)S(1)} %copy-done.6, bf16[2048,4096]{1,0:T(8,128)(2,1)} %gate.23, bf16[2048,4096]{1,0:T(8,128)(2,1)} %up.23, bf16[128,2048]{1,0:T(8,128)(2,1)S(1)} %copy-done), custom_call_target="tpu_custom_call" | custom-call | flops 6442450944 | bytes 16777216 | tf_op jit(solution)/shard_map/pallas_call | solution.py:89
  7.4 2.6 %collective-permute-start.1 = (bf16[2,128,512]{2,1,0:T(8,128)(2,1)S(1)}, bf16[2,128,512]{2,1,0:T(8,128)(2,1)S(1)}, u32[]{:S(2)}, u32[]{:S(2)}) collective-permute-start(bf16[2,128,512]{2,1,0:T(8,128)(2,1)S(1)} %get-tuple-element.181.rest_3_.rest_5_.rest_7_), channel_id=1, source_target_pairs={{0,1},{1,2},{2,3},{3,7},{7,6},{6,5},{5,4},{4,0},{8,9},{9,10},{10,1... | collective-permute-start | bytes 786440 | tf_op jit(solution)/shard_map/ppermute | solution.py:452
  10.0 5.1 %shard_map.74 = (bf16[2,128,512]{2,1,0:T(8,128)(2,1)S(1)}, bf16[2,128,512]{2,1,0:T(8,128)(2,1)S(1)}, bf16[128,2048]{1,0:T(8,128)(2,1)}, f32[8,128]{1,0:T(8,128)S(1)}) custom-call(s32[16,32]{1,0:T(8,128)S(1)} %copy-done.4, s32[16,32]{1,0:T(8,128)S(1)} %copy-done.6, bf16[2048,4096]{1,0:T(8,128)(2,1)} %gate.23, ...), custom_call_target="tpu_custom_call", output_to_operand_aliasing={{3}: (4, {})} | custom-call | flops 6442450944 | bytes 16777216 | tf_op jit(solution)/shard_map/pallas_call | solution.py:89
  19.3 4.5 %shard_map.76 = (bf16[2,128,512]{2,1,0:T(8,128)(2,1)S(1)}, bf16[2,128,512]{2,1,0:T(8,128)(2,1)S(1)}, f32[8,128]{1,0:T(8,128)S(1)}) custom-call(s32[16,32]{1,0:T(8,128)S(1)} %copy-done.5, s32[16,32]{1,0:T(8,128)S(1)} %copy-done.7, bf16[2048,4096]{1,0:T(8,128)(2,1)} %gate.23, bf16[2048,4096]{1,0:T(8,128)(2,1)} %up.23, ...), custom_call_target="tpu_custom_call", output_to_operand_aliasing={{2}: (4, {})} | custom-call | flops 6442450944 | bytes 16777216 | tf_op jit(solution)/shard_map/pallas_call | solution.py:89
  28.2 4.5 %shard_map.78 = (bf16[2,128,512]{2,1,0:T(8,128)(2,1)S(1)}, bf16[2,128,512]{2,1,0:T(8,128)(2,1)S(1)}, f32[8,128]{1,0:T(8,128)S(1)}) custom-call(s32[16,32]{1,0:T(8,128)S(1)} %copy-done.5, s32[16,32]{1,0:T(8,128)S(1)} %copy-done.7, bf16[2048,4096]{1,0:T(8,128)(2,1)} %gate.23, bf16[2048,4096]{1,0:T(8,128)(2,1)} %up.23, ...), custom_call_target="tpu_custom_call", output_to_operand_aliasing={{2}: (4, {})} | custom-call | flops 6442450944 | bytes 16777216 | tf_op jit(solution)/shard_map/pallas_call | solution.py:89
  39.6 4.6 %shard_map.81 = (bf16[2,256,512]{2,1,0:T(8,128)(2,1)S(1)}, bf16[2,256,512]{2,1,0:T(8,128)(2,1)S(1)}, f32[8,128]{1,0:T(8,128)S(1)}) custom-call(s32[16,32]{1,0:T(8,128)S(1)} %copy-done.5, s32[16,32]{1,0:T(8,128)S(1)} %copy-done.7, bf16[2048,4096]{1,0:T(8,128)(2,1)} %gate.23, bf16[2048,4096]{1,0:T(8,128)(2,1)} %up.23, ...), custom_call_target="tpu_custom_call", output_to_operand_aliasing={{2}: (4, {})} | custom-call | flops 6442450944 | bytes 16777216 | tf_op jit(solution)/shard_map/pallas_call | solution.py:89
  50.7 4.2 %collective-permute-done.12.left_in = bf16[2,128,512]{2,1,0:T(8,128)(2,1)} collective-permute-done((bf16[2,128,512]{2,1,0:T(8,128)(2,1)}, bf16[2,128,512]{2,1,0:T(8,128)(2,1)}, u32[]{:S(2)}, u32[]{:S(2)}) %collective-permute-start.12) | collective-permute-done | bytes 262176 | tf_op jit(solution)/shard_map/ppermute | solution.py:451
  62.8 4.6 %shard_map.86 = (bf16[2,256,512]{2,1,0:T(8,128)(2,1)S(1)}, bf16[2,256,512]{2,1,0:T(8,128)(2,1)S(1)}, f32[8,128]{1,0:T(8,128)S(1)}) custom-call(s32[16,32]{1,0:T(8,128)S(1)} %copy-done.5, s32[16,32]{1,0:T(8,128)S(1)} %copy-done.7, bf16[2048,4096]{1,0:T(8,128)(2,1)} %gate.23, bf16[2048,4096]{1,0:T(8,128)(2,1)} %up.23, ...), custom_call_target="tpu_custom_call", output_to_operand_aliasing={{2}: (4, {})} | custom-call | flops 6442450944 | bytes 16777216 | tf_op jit(solution)/shard_map/pallas_call | solution.py:89
  72.0 4.6 %shard_map.89 = (bf16[2,256,512]{2,1,0:T(8,128)(2,1)S(1)}, bf16[2,256,512]{2,1,0:T(8,128)(2,1)S(1)}, f32[8,128]{1,0:T(8,128)S(1)}) custom-call(s32[16,32]{1,0:T(8,128)S(1)} %copy-done.5, s32[16,32]{1,0:T(8,128)S(1)} %copy-done.7, bf16[2048,4096]{1,0:T(8,128)(2,1)} %gate.23, bf16[2048,4096]{1,0:T(8,128)(2,1)} %up.23, ...), custom_call_target="tpu_custom_call", output_to_operand_aliasing={{2}: (4, {})} | custom-call | flops 6442450944 | bytes 16777216 | tf_op jit(solution)/shard_map/pallas_call | solution.py:89
  81.4 6.4 %shard_map.92 = (f32[128,2048]{1,0:T(8,128)S(1)}, f32[8,128]{1,0:T(8,128)S(1)}) custom-call(s32[1]{0:T(128)} %bitcast.z_ref, s32[32,16]{1,0:T(8,128)S(1)} %copy.63.mask, f32[8,128]{1,0:T(8,128)S(1)} %get-tuple-element.234.tok, bf16[4096,2048]{1,0:T(8,128)(2,1)} %down.11, bf16[128,512]{1,0:T(8,128)(2,1)S(1)} %copy-done.11, ...), custom_call_target="tpu_custom_call", output_to_operand_aliasing={{1}: (2, {})} | custom-call | flops 6442450944 | bytes 16777216 | tf_op jit(solution)/shard_map/pallas_call | solution.py:302
  92.1 4.6 %shard_map.95 = (bf16[2,256,512]{2,1,0:T(8,128)(2,1)S(1)}, bf16[2,256,512]{2,1,0:T(8,128)(2,1)S(1)}, f32[8,128]{1,0:T(8,128)S(1)}) custom-call(s32[16,32]{1,0:T(8,128)S(1)} %copy-done.5, s32[16,32]{1,0:T(8,128)S(1)} %copy-done.7, bf16[2048,4096]{1,0:T(8,128)(2,1)} %gate.23, bf16[2048,4096]{1,0:T(8,128)(2,1)} %up.23, ...), custom_call_target="tpu_custom_call", output_to_operand_aliasing={{2}: (4, {})} | custom-call | flops 6442450944 | bytes 16777216 | tf_op jit(solution)/shard_map/pallas_call | solution.py:89
  97.7 2.0 collective-permute-start.33
  101.2 5.3 %shard_map.98 = (bf16[128,2048]{1,0:T(8,128)(2,1)S(1)}, f32[8,128]{1,0:T(8,128)S(1)}) custom-call(s32[1]{0:T(128)} %bitcast.z_ref, s32[32,16]{1,0:T(8,128)S(1)} %copy.63.mask, f32[8,128]{1,0:T(8,128)S(1)} %get-tuple-element.252.tok, bf16[4096,2048]{1,0:T(8,128)(2,1)} %down.11, ...), custom_call_target="tpu_custom_call", output_to_operand_aliasing={{1}: (2, {})} | custom-call | flops 6442450944 | bytes 16777216 | tf_op jit(solution)/shard_map/pallas_call | solution.py:302
  106.9 2.0 collective-permute-start.38
  111.0 4.5 %shard_map.101 = (bf16[2,128,512]{2,1,0:T(8,128)(2,1)S(1)}, bf16[2,128,512]{2,1,0:T(8,128)(2,1)S(1)}, f32[8,128]{1,0:T(8,128)S(1)}) custom-call(s32[16,32]{1,0:T(8,128)S(1)} %copy-done.5, s32[16,32]{1,0:T(8,128)S(1)} %copy-done.7, bf16[2048,4096]{1,0:T(8,128)(2,1)} %gate.23, bf16[2048,4096]{1,0:T(8,128)(2,1)} %up.23, ...), custom_call_target="tpu_custom_call", output_to_operand_aliasing={{2}: (4, {})} | custom-call | flops 6442450944 | bytes 16777216 | tf_op jit(solution)/shard_map/pallas_call | solution.py:89
  119.9 4.5 %shard_map.104 = (bf16[2,128,512]{2,1,0:T(8,128)(2,1)S(1)}, bf16[2,128,512]{2,1,0:T(8,128)(2,1)S(1)}, f32[8,128]{1,0:T(8,128)S(1)}) custom-call(s32[16,32]{1,0:T(8,128)S(1)} %copy-done.5, s32[16,32]{1,0:T(8,128)S(1)} %copy-done.7, bf16[2048,4096]{1,0:T(8,128)(2,1)} %gate.23, bf16[2048,4096]{1,0:T(8,128)(2,1)} %up.23, ...), custom_call_target="tpu_custom_call", output_to_operand_aliasing={{2}: (4, {})} | custom-call | flops 6442450944 | bytes 16777216 | tf_op jit(solution)/shard_map/pallas_call | solution.py:89
  128.8 4.5 %shard_map.107 = (bf16[2,128,512]{2,1,0:T(8,128)(2,1)S(1)}, bf16[2,128,512]{2,1,0:T(8,128)(2,1)S(1)}, f32[8,128]{1,0:T(8,128)S(1)}) custom-call(s32[16,32]{1,0:T(8,128)S(1)} %copy-done.5, s32[16,32]{1,0:T(8,128)S(1)} %copy-done.7, bf16[2048,4096]{1,0:T(8,128)(2,1)} %gate.23, bf16[2048,4096]{1,0:T(8,128)(2,1)} %up.23, ...), custom_call_target="tpu_custom_call", output_to_operand_aliasing={{2}: (4, {})} | custom-call | flops 6442450944 | bytes 16777216 | tf_op jit(solution)/shard_map/pallas_call | solution.py:89
  137.8 6.1 %shard_map.110 = (f32[256,2048]{1,0:T(8,128)S(1)}, f32[8,128]{1,0:T(8,128)S(1)}) custom-call(s32[1]{0:T(128)} %bitcast.z_ref, s32[32,16]{1,0:T(8,128)S(1)} %copy.63.mask, f32[8,128]{1,0:T(8,128)S(1)} %get-tuple-element.292.tok, bf16[4096,2048]{1,0:T(8,128)(2,1)} %down.11, ...), custom_call_target="tpu_custom_call", output_to_operand_aliasing={{1}: (2, {})} | custom-call | flops 6442450944 | bytes 16777216 | tf_op jit(solution)/shard_map/pallas_call | solution.py:302
  148.5 4.5 %shard_map.113 = (bf16[2,128,512]{2,1,0:T(8,128)(2,1)S(1)}, bf16[2,128,512]{2,1,0:T(8,128)(2,1)S(1)}, f32[8,128]{1,0:T(8,128)S(1)}) custom-call(s32[16,32]{1,0:T(8,128)S(1)} %copy-done.5, s32[16,32]{1,0:T(8,128)S(1)} %copy-done.7, bf16[2048,4096]{1,0:T(8,128)(2,1)} %gate.23, bf16[2048,4096]{1,0:T(8,128)(2,1)} %up.23, ...), custom_call_target="tpu_custom_call", output_to_operand_aliasing={{2}: (4, {})} | custom-call | flops 6442450944 | bytes 16777216 | tf_op jit(solution)/shard_map/pallas_call | solution.py:89
  157.4 4.2 %collective-permute-done.57.left_in = bf16[2,128,512]{2,1,0:T(8,128)(2,1)S(1)} collective-permute-done((bf16[2,128,512]{2,1,0:T(8,128)(2,1)S(1)}, bf16[2,128,512]{2,1,0:T(8,128)(2,1)S(1)}, u32[]{:S(2)}, u32[]{:S(2)}) %collective-permute-start.57) | collective-permute-done | bytes 262176 | tf_op jit(solution)/shard_map/ppermute | solution.py:451
  162.5 2.5 %collective-permute-start.62 = (bf16[2,128,512]{2,1,0:T(8,128)(2,1)S(1)}, bf16[2,128,512]{2,1,0:T(8,128)(2,1)S(1)}, u32[]{:S(2)}, u32[]{:S(2)}) collective-permute-start(bf16[2,128,512]{2,1,0:T(8,128)(2,1)S(1)} %get-tuple-element.321), channel_id=1, source_target_pairs={{0,1},{1,2},{2,3},{3,7},{7,6},{6,5},{5,4},{4,0},{8,9},{9,10},{10,1... | collective-permute-start | bytes 786440 | tf_op jit(solution)/shard_map/ppermute | solution.py:452
  165.0 2.4 %collective-permute-start.63 = (bf16[128,512]{1,0:T(8,128)(2,1)S(1)}, bf16[128,512]{1,0:T(8,128)(2,1)S(1)}, u32[]{:S(2)}, u32[]{:S(2)}) collective-permute-start(bf16[128,512]{1,0:T(8,128)(2,1)S(1)} %get-tuple-element.324.rest_14_.rest_28_.rest_2_.rest_8_), channel_id=1, source_target_pairs={{0,1},{1,2},{2,3},{3,7},{7,6},{6,5},{5,4},{4,0},{8,9},{9,10},{10,1... | collective-permute-start | bytes 393224 | tf_op jit(solution)/shard_map/ppermute | solution.py:457
  167.3 2.7 %collective-permute-done.61.left_in = bf16[2,128,512]{2,1,0:T(8,128)(2,1)S(1)} collective-permute-done((bf16[2,128,512]{2,1,0:T(8,128)(2,1)S(1)}, bf16[2,128,512]{2,1,0:T(8,128)(2,1)S(1)}, u32[]{:S(2)}, u32[]{:S(2)}) %collective-permute-start.61) | collective-permute-done | bytes 262176 | tf_op jit(solution)/shard_map/ppermute | solution.py:451
  172.0 2.4 %collective-permute-start.66 = (bf16[2,128,512]{2,1,0:T(8,128)(2,1)S(1)}, bf16[2,128,512]{2,1,0:T(8,128)(2,1)S(1)}, u32[]{:S(2)}, u32[]{:S(2)}) collective-permute-start(bf16[2,128,512]{2,1,0:T(8,128)(2,1)S(1)} %get-tuple-element.332), channel_id=1, source_target_pairs={{0,1},{1,2},{2,3},{3,7},{7,6},{6,5},{5,4},{4,0},{8,9},{9,10},{10,1... | collective-permute-start | bytes 786440 | tf_op jit(solution)/shard_map/ppermute | solution.py:452
  174.5 2.4 %collective-permute-start.67 = (bf16[128,512]{1,0:T(8,128)(2,1)S(1)}, bf16[128,512]{1,0:T(8,128)(2,1)S(1)}, u32[]{:S(2)}, u32[]{:S(2)}) collective-permute-start(bf16[128,512]{1,0:T(8,128)(2,1)S(1)} %get-tuple-element.327.rest_30_.rest_4_.rest_10_.rest_0_), channel_id=1, source_target_pairs={{0,1},{1,2},{2,3},{3,7},{7,6},{6,5},{5,4},{4,0},{8,9},{9,10},{10,1... | collective-permute-start | bytes 393224 | tf_op jit(solution)/shard_map/ppermute | solution.py:457
  176.9 6.1 %shard_map.120 = (bf16[128,2048]{1,0:T(8,128)(2,1)S(1)}, bf16[128,2048]{1,0:T(8,128)(2,1)S(1)}, f32[8,128]{1,0:T(8,128)S(1)}) custom-call(s32[1]{0:T(128)} %bitcast.z_ref, s32[32,16]{1,0:T(8,128)S(1)} %copy.63.mask, f32[8,128]{1,0:T(8,128)S(1)} %get-tuple-element.326.tok, bf16[4096,2048]{1,0:T(8,128)(2,1)} %down.11, ...), custom_call_target="tpu_custom_call", output_to_operand_aliasing={{2}: (2, {})} | custom-call | flops 6442450944 | bytes 16777216 | tf_op jit(solution)/shard_map/pallas_call | solution.py:302
  185.3 3.3 %collective-permute-done.71.rest_0_ = bf16[128,512]{1,0:T(8,128)(2,1)S(1)} collective-permute-done((bf16[128,512]{1,0:T(8,128)(2,1)S(1)}, bf16[128,512]{1,0:T(8,128)(2,1)S(1)}, u32[]{:S(2)}, u32[]{:S(2)}) %collective-permute-start.71) | collective-permute-done | bytes 131104 | tf_op jit(solution)/shard_map/ppermute | solution.py:457
  191.1 5.1 %shard_map.125 = (f32[128,2048]{1,0:T(8,128)S(1)}, f32[8,128]{1,0:T(8,128)S(1)}) custom-call(s32[1]{0:T(128)} %bitcast.z_ref, s32[32,16]{1,0:T(8,128)S(1)} %copy.63.mask, f32[8,128]{1,0:T(8,128)S(1)} %get-tuple-element.342.tok, bf16[4096,2048]{1,0:T(8,128)(2,1)} %down.11, ...), custom_call_target="tpu_custom_call", output_to_operand_aliasing={{1}: (2, {})} | custom-call | flops 6442450944 | bytes 16777216 | tf_op jit(solution)/shard_map/pallas_call | solution.py:302
  196.2 2.0 collective-permute-start.75
  200.8 2.4 %collective-permute-done.76.rest_15_ = bf16[128,512]{1,0:T(8,128)(2,1)S(1)} collective-permute-done((bf16[128,512]{1,0:T(8,128)(2,1)S(1)}, bf16[128,512]{1,0:T(8,128)(2,1)S(1)}, u32[]{:S(2)}, u32[]{:S(2)}) %collective-permute-start.76) | collective-permute-done | bytes 131104 | tf_op jit(solution)/shard_map/ppermute | solution.py:456
  203.3 5.1 %shard_map.127 = (bf16[128,2048]{1,0:T(8,128)(2,1)S(1)}, f32[8,128]{1,0:T(8,128)S(1)}) custom-call(s32[1]{0:T(128)} %bitcast.z_ref, s32[32,16]{1,0:T(8,128)S(1)} %copy.63.mask, f32[8,128]{1,0:T(8,128)S(1)} %get-tuple-element.346.tok, bf16[4096,2048]{1,0:T(8,128)(2,1)} %down.11, ...), custom_call_target="tpu_custom_call", output_to_operand_aliasing={{1}: (2, {})} | custom-call | flops 6442450944 | bytes 16777216 | tf_op jit(solution)/shard_map/pallas_call | solution.py:302
  208.4 2.7 %collective-permute-done.70 = bf16[128,2048]{1,0:T(8,128)(2,1)S(1)} collective-permute-done((bf16[128,2048]{1,0:T(8,128)(2,1)S(1)}, bf16[128,2048]{1,0:T(8,128)(2,1)S(1)}, u32[]{:S(2)}, u32[]{:S(2)}) %collective-permute-start.70) | collective-permute-done | bytes 524320 | tf_op jit(solution)/shard_map/ppermute | solution.py:368
  (207 shorter events, 85.0 us)
Async XLA Ops:
  6.9 10.2 %collective-permute-start = (bf16[2,128,512]{2,1,0:T(8,128)(2,1)S(1)}, bf16[2,128,512]{2,1,0:T(8,128)(2,1)S(1)}, u32[]{:S(2)}, u32[]{:S(2)}) collective-permute-start(bf16[2,128,512]{2,1,0:T(8,128)(2,1)S(1)} %get-tuple-element.180.rest_0_), channel_id=1, source_target_pairs={{1,0},{2,1},{3,2},{7,3},{6,7},{5,6},{4,5},{0,4},{9,8},{10,9},{11,1... | collective-permute-start | bytes 786440 | tf_op jit(solution)/shard_map/ppermute | solution.py:451
  7.4 9.8 %collective-permute-start.1 = (bf16[2,128,512]{2,1,0:T(8,128)(2,1)S(1)}, bf16[2,128,512]{2,1,0:T(8,128)(2,1)S(1)}, u32[]{:S(2)}, u32[]{:S(2)}) collective-permute-start(bf16[2,128,512]{2,1,0:T(8,128)(2,1)S(1)} %get-tuple-element.181.rest_3_.rest_5_.rest_7_), channel_id=1, source_target_pairs={{0,1},{1,2},{2,3},{3,7},{7,6},{6,5},{5,4},{4,0},{8,9},{9,10},{10,1... | collective-permute-start | bytes 786440 | tf_op jit(solution)/shard_map/ppermute | solution.py:452
  15.1 24.5 %collective-permute-start.6 = (bf16[128,2048]{1,0:T(8,128)(2,1)}, bf16[128,2048]{1,0:T(8,128)(2,1)S(1)}, u32[]{:S(2)}, u32[]{:S(2)}) collective-permute-start(bf16[128,2048]{1,0:T(8,128)(2,1)} %get-tuple-element.199), channel_id=1, source_target_pairs={{8,0},{12,4},{0,8},{4,12},{9,1},{13,5},{1,9},{5,13},{10,2},{14,6},... | collective-permute-start | bytes 1572872 | tf_op jit(solution)/shard_map/ppermute | solution.py:368
  17.1 22.5 %collective-permute-start.7 = (bf16[128,2048]{1,0:T(8,128)(2,1)}, bf16[128,2048]{1,0:T(8,128)(2,1)S(1)}, u32[]{:S(2)}, u32[]{:S(2)}) collective-permute-start(bf16[128,2048]{1,0:T(8,128)(2,1)} %get-tuple-element.199), channel_id=1, source_target_pairs={{12,0},{8,4},{4,8},{0,12},{13,1},{9,5},{5,9},{1,13},{14,2},{10,6},... | collective-permute-start | bytes 1572872 | tf_op jit(solution)/shard_map/ppermute | solution.py:368
  35.0 9.3 %collective-permute-start.8 = (bf16[2,128,512]{2,1,0:T(8,128)(2,1)S(1)}, bf16[2,128,512]{2,1,0:T(8,128)(2,1)S(1)}, u32[]{:S(2)}, u32[]{:S(2)}) collective-permute-start(bf16[2,128,512]{2,1,0:T(8,128)(2,1)S(1)} %get-tuple-element.201), channel_id=1, source_target_pairs={{1,0},{2,1},{3,2},{7,3},{6,7},{5,6},{4,5},{0,4},{9,8},{10,9},{11,1... | collective-permute-start | bytes 786440 | tf_op jit(solution)/shard_map/ppermute | solution.py:451
  37.7 10.3 %collective-permute-start.10 = (bf16[128,512]{1,0:T(8,128)(2,1)S(1)}, bf16[128,512]{1,0:T(8,128)(2,1)S(1)}, u32[]{:S(2)}, u32[]{:S(2)}) collective-permute-start(bf16[128,512]{1,0:T(8,128)(2,1)S(1)} %get-tuple-element.207.rest_0_), channel_id=1, source_target_pairs={{0,1},{1,2},{2,3},{3,7},{7,6},{6,5},{5,4},{4,0},{8,9},{9,10},{10,1... | collective-permute-start | bytes 393224 | tf_op jit(solution)/shard_map/ppermute | solution.py:457
  45.5 9.5 %collective-permute-start.12 = (bf16[2,128,512]{2,1,0:T(8,128)(2,1)}, bf16[2,128,512]{2,1,0:T(8,128)(2,1)}, u32[]{:S(2)}, u32[]{:S(2)}) collective-permute-start(bf16[2,128,512]{2,1,0:T(8,128)(2,1)} %get-tuple-element.210), channel_id=1, source_target_pairs={{1,0},{2,1},{3,2},{7,3},{6,7},{5,6},{4,5},{0,4},{9,8},{10,9},{11,1... | collective-permute-start | bytes 786440 | tf_op jit(solution)/shard_map/ppermute | solution.py:451
  48.7 11.1 %collective-permute-start.14 = (bf16[128,512]{1,0:T(8,128)(2,1)}, bf16[128,512]{1,0:T(8,128)(2,1)}, u32[]{:S(2)}, u32[]{:S(2)}) collective-permute-start(bf16[128,512]{1,0:T(8,128)(2,1)} %get-tuple-element.214.rest_2_.rest_8_), channel_id=1, source_target_pairs={{0,1},{1,2},{2,3},{3,7},{7,6},{6,5},{5,4},{4,0},{8,9},{9,10},{10,1... | collective-permute-start | bytes 393224 | tf_op jit(solution)/shard_map/ppermute | solution.py:457
  50.7 9.1 %collective-permute-start.15 = (bf16[128,512]{1,0:T(8,128)(2,1)}, bf16[128,512]{1,0:T(8,128)(2,1)}, u32[]{:S(2)}, u32[]{:S(2)}) collective-permute-start(bf16[128,512]{1,0:T(8,128)(2,1)} %get-tuple-element.215.rest_3_.rest_9_), channel_id=1, source_target_pairs={{1,0},{2,1},{3,2},{7,3},{6,7},{5,6},{4,5},{0,4},{9,8},{10,9},{11,1... | collective-permute-start | bytes 393224 | tf_op jit(solution)/shard_map/ppermute | solution.py:456
  50.7 60.3 %collective-permute-start.36 = (bf16[128,2048]{1,0:T(8,128)(2,1)}, bf16[128,2048]{1,0:T(8,128)(2,1)S(1)}, u32[]{:S(2)}, u32[]{:S(2)}) collective-permute-start(bf16[128,2048]{1,0:T(8,128)(2,1)} %get-tuple-element.199), channel_id=1, source_target_pairs={{4,0},{0,4},{12,8},{8,12},{5,1},{1,5},{13,9},{9,13},{6,2},{2,6},{1... | collective-permute-start | bytes 1572872 | tf_op jit(solution)/shard_map/ppermute | solution.py:368
  57.3 10.1 %collective-permute-start.16 = (bf16[2,128,512]{2,1,0:T(8,128)(2,1)S(1)}, bf16[2,128,512]{2,1,0:T(8,128)(2,1)S(1)}, u32[]{:S(2)}, u32[]{:S(2)}) collective-permute-start(bf16[2,128,512]{2,1,0:T(8,128)(2,1)S(1)} %get-tuple-element.218), channel_id=1, source_target_pairs={{1,0},{2,1},{3,2},{7,3},{6,7},{5,6},{4,5},{0,4},{9,8},{10,9},{11,1... | collective-permute-start | bytes 786440 | tf_op jit(solution)/shard_map/ppermute | solution.py:451
  58.3 9.1 %collective-permute-start.17 = (bf16[2,128,512]{2,1,0:T(8,128)(2,1)S(1)}, bf16[2,128,512]{2,1,0:T(8,128)(2,1)S(1)}, u32[]{:S(2)}, u32[]{:S(2)}) collective-permute-start(bf16[2,128,512]{2,1,0:T(8,128)(2,1)S(1)} %get-tuple-element.219), channel_id=1, source_target_pairs={{0,1},{1,2},{2,3},{3,7},{7,6},{6,5},{5,4},{4,0},{8,9},{9,10},{10,1... | collective-permute-start | bytes 786440 | tf_op jit(solution)/shard_map/ppermute | solution.py:452
  60.8 9.0 %collective-permute-start.18 = (bf16[128,512]{1,0:T(8,128)(2,1)S(1)}, bf16[128,512]{1,0:T(8,128)(2,1)S(1)}, u32[]{:S(2)}, u32[]{:S(2)}) collective-permute-start(bf16[128,512]{1,0:T(8,128)(2,1)S(1)} %get-tuple-element.224.rest_4_.rest_10_.rest_0_), channel_id=1, source_target_pairs={{0,1},{1,2},{2,3},{3,7},{7,6},{6,5},{5,4},{4,0},{8,9},{9,10},{10,1... | collective-permute-start | bytes 393224 | tf_op jit(solution)/shard_map/ppermute | solution.py:457
  70.0 9.3 %collective-permute-start.22 = (bf16[128,512]{1,0:T(8,128)(2,1)S(1)}, bf16[128,512]{1,0:T(8,128)(2,1)S(1)}, u32[]{:S(2)}, u32[]{:S(2)}) collective-permute-start(bf16[128,512]{1,0:T(8,128)(2,1)S(1)} %get-tuple-element.232.rest_6_.rest_12_.rest_2_.rest_8_), channel_id=1, source_target_pairs={{0,1},{1,2},{2,3},{3,7},{7,6},{6,5},{5,4},{4,0},{8,9},{9,10},{10,1... | collective-permute-start | bytes 393224 | tf_op jit(solution)/shard_map/ppermute | solution.py:457
  77.0 10.8 %collective-permute-start.24 = (bf16[2,128,512]{2,1,0:T(8,128)(2,1)S(1)}, bf16[2,128,512]{2,1,0:T(8,128)(2,1)S(1)}, u32[]{:S(2)}, u32[]{:S(2)}) collective-permute-start(bf16[2,128,512]{2,1,0:T(8,128)(2,1)S(1)} %get-tuple-element.238), channel_id=1, source_target_pairs={{1,0},{2,1},{3,2},{7,3},{6,7},{5,6},{4,5},{0,4},{9,8},{10,9},{11,1... | collective-permute-start | bytes 786440 | tf_op jit(solution)/shard_map/ppermute | solution.py:451
  78.1 9.7 %collective-permute-start.25 = (bf16[2,128,512]{2,1,0:T(8,128)(2,1)S(1)}, bf16[2,128,512]{2,1,0:T(8,128)(2,1)S(1)}, u32[]{:S(2)}, u32[]{:S(2)}) collective-permute-start(bf16[2,128,512]{2,1,0:T(8,128)(2,1)S(1)} %get-tuple-element.239), channel_id=1, source_target_pairs={{0,1},{1,2},{2,3},{3,7},{7,6},{6,5},{5,4},{4,0},{8,9},{9,10},{10,1... | collective-permute-start | bytes 786440 | tf_op jit(solution)/shard_map/ppermute | solution.py:452
  79.4 10.8 %collective-permute-start.26 = (bf16[128,512]{1,0:T(8,128)(2,1)S(1)}, bf16[128,512]{1,0:T(8,128)(2,1)S(1)}, u32[]{:S(2)}, u32[]{:S(2)}) collective-permute-start(bf16[128,512]{1,0:T(8,128)(2,1)S(1)} %get-tuple-element.235.rest_14_.rest_4_.rest_10_.rest_0_), channel_id=1, source_target_pairs={{0,1},{1,2},{2,3},{3,7},{7,6},{6,5},{5,4},{4,0},{8,9},{9,10},{10,1... | collective-permute-start | bytes 393224 | tf_op jit(solution)/shard_map/ppermute | solution.py:457
  88.2 9.1 %collective-permute-start.28 = (bf16[2,128,512]{2,1,0:T(8,128)(2,1)S(1)}, bf16[2,128,512]{2,1,0:T(8,128)(2,1)S(1)}, u32[]{:S(2)}, u32[]{:S(2)}) collective-permute-start(bf16[2,128,512]{2,1,0:T(8,128)(2,1)S(1)} %get-tuple-element.246), channel_id=1, source_target_pairs={{1,0},{2,1},{3,2},{7,3},{6,7},{5,6},{4,5},{0,4},{9,8},{10,9},{11,1... | collective-permute-start | bytes 786440 | tf_op jit(solution)/shard_map/ppermute | solution.py:451
  88.2 9.1 %collective-permute-start.29 = (bf16[2,128,512]{2,1,0:T(8,128)(2,1)S(1)}, bf16[2,128,512]{2,1,0:T(8,128)(2,1)S(1)}, u32[]{:S(2)}, u32[]{:S(2)}) collective-permute-start(bf16[2,128,512]{2,1,0:T(8,128)(2,1)S(1)} %get-tuple-element.247), channel_id=1, source_target_pairs={{0,1},{1,2},{2,3},{3,7},{7,6},{6,5},{5,4},{4,0},{8,9},{9,10},{10,1... | collective-permute-start | bytes 786440 | tf_op jit(solution)/shard_map/ppermute | solution.py:452
  90.3 9.5 %collective-permute-start.30 = (bf16[128,512]{1,0:T(8,128)(2,1)S(1)}, bf16[128,512]{1,0:T(8,128)(2,1)S(1)}, u32[]{:S(2)}, u32[]{:S(2)}) collective-permute-start(bf16[128,512]{1,0:T(8,128)(2,1)S(1)} %get-tuple-element.250.rest_6_.rest_12_.rest_2_.rest_16_), channel_id=1, source_target_pairs={{0,1},{1,2},{2,3},{3,7},{7,6},{6,5},{5,4},{4,0},{8,9},{9,10},{10,1... | collective-permute-start | bytes 393224 | tf_op jit(solution)/shard_map/ppermute | solution.py:457
  99.8 9.1 %collective-permute-start.34 = (bf16[128,512]{1,0:T(8,128)(2,1)S(1)}, bf16[128,512]{1,0:T(8,128)(2,1)S(1)}, u32[]{:S(2)}, u32[]{:S(2)}) collective-permute-start(bf16[128,512]{1,0:T(8,128)(2,1)S(1)} %get-tuple-element.253.rest_14_.rest_4_.rest_8_.rest_18_), channel_id=1, source_target_pairs={{0,1},{1,2},{2,3},{3,7},{7,6},{6,5},{5,4},{4,0},{8,9},{9,10},{10,1... | collective-permute-start | bytes 393224 | tf_op jit(solution)/shard_map/ppermute | solution.py:457
  106.9 9.0 %collective-permute-start.37 = (bf16[2,128,512]{2,1,0:T(8,128)(2,1)S(1)}, bf16[2,128,512]{2,1,0:T(8,128)(2,1)S(1)}, u32[]{:S(2)}, u32[]{:S(2)}) collective-permute-start(bf16[2,128,512]{2,1,0:T(8,128)(2,1)S(1)} %get-tuple-element.266), channel_id=1, source_target_pairs={{1,0},{2,1},{3,2},{7,3},{6,7},{5,6},{4,5},{0,4},{9,8},{10,9},{11,1... | collective-permute-start | bytes 786440 | tf_op jit(solution)/shard_map/ppermute | solution.py:451
  109.0 9.3 %collective-permute-start.39 = (bf16[128,512]{1,0:T(8,128)(2,1)S(1)}, bf16[128,512]{1,0:T(8,128)(2,1)S(1)}, u32[]{:S(2)}, u32[]{:S(2)}) collective-permute-start(bf16[128,512]{1,0:T(8,128)(2,1)S(1)} %get-tuple-element.270.rest_6_.rest_10_.rest_20_.rest_24_), channel_id=1, source_target_pairs={{0,1},{1,2},{2,3},{3,7},{7,6},{6,5},{5,4},{4,0},{8,9},{9,10},{10,1... | collective-permute-start | bytes 393224 | tf_op jit(solution)/shard_map/ppermute | solution.py:457
  133.8 10.1 %collective-permute-start.49 = (bf16[2,128,512]{2,1,0:T(8,128)(2,1)S(1)}, bf16[2,128,512]{2,1,0:T(8,128)(2,1)S(1)}, u32[]{:S(2)}, u32[]{:S(2)}) collective-permute-start(bf16[2,128,512]{2,1,0:T(8,128)(2,1)S(1)} %get-tuple-element.296), channel_id=1, source_target_pairs={{1,0},{2,1},{3,2},{7,3},{6,7},{5,6},{4,5},{0,4},{9,8},{10,9},{11,1... | collective-permute-start | bytes 786440 | tf_op jit(solution)/shard_map/ppermute | solution.py:451
  133.8 10.1 %collective-permute-start.50 = (bf16[2,128,512]{2,1,0:T(8,128)(2,1)S(1)}, bf16[2,128,512]{2,1,0:T(8,128)(2,1)S(1)}, u32[]{:S(2)}, u32[]{:S(2)}) collective-permute-start(bf16[2,128,512]{2,1,0:T(8,128)(2,1)S(1)} %get-tuple-element.297), channel_id=1, source_target_pairs={{0,1},{1,2},{2,3},{3,7},{7,6},{6,5},{5,4},{4,0},{8,9},{9,10},{10,1... | collective-permute-start | bytes 786440 | tf_op jit(solution)/shard_map/ppermute | solution.py:452
  135.8 10.7 %collective-permute-start.51 = (bf16[128,512]{1,0:T(8,128)(2,1)S(1)}, bf16[128,512]{1,0:T(8,128)(2,1)S(1)}, u32[]{:S(2)}, u32[]{:S(2)}) collective-permute-start(bf16[128,512]{1,0:T(8,128)(2,1)S(1)} %get-tuple-element.293.rest_30_.rest_4_.rest_8_.rest_18_), channel_id=1, source_target_pairs={{0,1},{1,2},{2,3},{3,7},{7,6},{6,5},{5,4},{4,0},{8,9},{9,10},{10,1... | collective-permute-start | bytes 393224 | tf_op jit(solution)/shard_map/ppermute | solution.py:457
  155.5 9.5 %collective-permute-start.59 = (bf16[128,512]{1,0:T(8,128)(2,1)S(1)}, bf16[128,512]{1,0:T(8,128)(2,1)S(1)}, u32[]{:S(2)}, u32[]{:S(2)}) collective-permute-start(bf16[128,512]{1,0:T(8,128)(2,1)S(1)} %get-tuple-element.317.rest_12_.rest_22_.rest_26_.rest_0_), channel_id=1, source_target_pairs={{0,1},{1,2},{2,3},{3,7},{7,6},{6,5},{5,4},{4,0},{8,9},{9,10},{10,1... | collective-permute-start | bytes 393224 | tf_op jit(solution)/shard_map/ppermute | solution.py:457
  162.5 9.2 %collective-permute-start.62 = (bf16[2,128,512]{2,1,0:T(8,128)(2,1)S(1)}, bf16[2,128,512]{2,1,0:T(8,128)(2,1)S(1)}, u32[]{:S(2)}, u32[]{:S(2)}) collective-permute-start(bf16[2,128,512]{2,1,0:T(8,128)(2,1)S(1)} %get-tuple-element.321), channel_id=1, source_target_pairs={{0,1},{1,2},{2,3},{3,7},{7,6},{6,5},{5,4},{4,0},{8,9},{9,10},{10,1... | collective-permute-start | bytes 786440 | tf_op jit(solution)/shard_map/ppermute | solution.py:452
  165.0 9.5 %collective-permute-start.63 = (bf16[128,512]{1,0:T(8,128)(2,1)S(1)}, bf16[128,512]{1,0:T(8,128)(2,1)S(1)}, u32[]{:S(2)}, u32[]{:S(2)}) collective-permute-start(bf16[128,512]{1,0:T(8,128)(2,1)S(1)} %get-tuple-element.324.rest_14_.rest_28_.rest_2_.rest_8_), channel_id=1, source_target_pairs={{0,1},{1,2},{2,3},{3,7},{7,6},{6,5},{5,4},{4,0},{8,9},{9,10},{10,1... | collective-permute-start | bytes 393224 | tf_op jit(solution)/shard_map/ppermute | solution.py:457
  172.0 11.1 %collective-permute-start.65 = (bf16[2,128,512]{2,1,0:T(8,128)(2,1)S(1)}, bf16[2,128,512]{2,1,0:T(8,128)(2,1)S(1)}, u32[]{:S(2)}, u32[]{:S(2)}) collective-permute-start(bf16[2,128,512]{2,1,0:T(8,128)(2,1)S(1)} %get-tuple-element.331), channel_id=1, source_target_pairs={{1,0},{2,1},{3,2},{7,3},{6,7},{5,6},{4,5},{0,4},{9,8},{10,9},{11,1... | collective-permute-start | bytes 786440 | tf_op jit(solution)/shard_map/ppermute | solution.py:451
  172.0 11.0 %collective-permute-start.66 = (bf16[2,128,512]{2,1,0:T(8,128)(2,1)S(1)}, bf16[2,128,512]{2,1,0:T(8,128)(2,1)S(1)}, u32[]{:S(2)}, u32[]{:S(2)}) collective-permute-start(bf16[2,128,512]{2,1,0:T(8,128)(2,1)S(1)} %get-tuple-element.332), channel_id=1, source_target_pairs={{0,1},{1,2},{2,3},{3,7},{7,6},{6,5},{5,4},{4,0},{8,9},{9,10},{10,1... | collective-permute-start | bytes 786440 | tf_op jit(solution)/shard_map/ppermute | solution.py:452
  198.3 12.8 %collective-permute-start.70 = (bf16[128,2048]{1,0:T(8,128)(2,1)S(1)}, bf16[128,2048]{1,0:T(8,128)(2,1)S(1)}, u32[]{:S(2)}, u32[]{:S(2)}) collective-permute-start(bf16[128,2048]{1,0:T(8,128)(2,1)S(1)} %get-tuple-element.338), channel_id=1, source_target_pairs={{0,8},{4,12},{8,0},{12,4},{1,9},{5,13},{9,1},{13,5},{2,10},{6,14},... | collective-permute-start | bytes 1572872 | tf_op jit(solution)/shard_map/ppermute | solution.py:368
  (59 other events, 425.1 us)
where the time goes:
time: 212 us
  Pallas kernels  98.8 us (47%)
  starting transfers between devices  78.9 us (37%)
  waiting for transfers between devices  29.1 us (14%)
  local copies, waits for them, and re-layouts  3.5 us (2%)
    pallas_call x12, Pallas kernels, partials(): pl.pallas_call(functools.partial(partial_kernel, depth // gm.shape[0], un...  54.6 us
    ppermute x18, starting transfers between devices, shards(): right_got[t] = lax.ppermute(sums[1], ('row', 'col'), to_right)  34.6 us
    ppermute x18, starting transfers between devices, shards(): right_came[t] = lax.ppermute(right_on[t], ('row', 'col'), to_right)  34.1 us
    pallas_call x6, Pallas kernels, project(): pl.pallas_call(functools.partial(project_kernel, tuple((h[:3] for h in hi...  33.9 us
    ppermute x18, waiting for transfers between devices, shards(): left_got[t] = lax.ppermute(sums[0], ('row', 'col'), to_left)  14.9 us
    pallas_call x18, Pallas kernels, sum_step(): pl.pallas_call(functools.partial(sum_kernel, own, n_col, goes_on, ends),...  7.84 us
    ppermute x18, starting transfers between devices, shards(): left_got[t] = lax.ppermute(sums[0], ('row', 'col'), to_left)  6.43 us
    ppermute x18, waiting for transfers between devices, shards(): right_came[t] = lax.ppermute(right_on[t], ('row', 'col'), to_right)  4.32 us
  transfers between devices with their start and end apart: 78, of which 18 were waited for; matrix products, arithmetic and copies ran while one was open for 0% of the time, Pallas kernels for 44%

commit v1 on v0

--- a/solution.py
+++ b/solution.py
@@ -27,7 +27,7 @@
     return jnp.concatenate(strips, axis=0)
 
 
-def partial_kernel(edge, unit, first, hand_on, gm_hbm, um_hbm, gate, up, *rest):
+def partial_kernel(edge, unit, first, hand_on, unroll, gm_hbm, um_hbm, gate, up, *rest):
     rest, (w, masks, sems, mask_sems) = rest[:-4], rest[-4:]
     *rest, tok_out = rest
     if hand_on:
@@ -75,19 +75,19 @@
             ).astype(out.dtype)
             return 0
 
-        if len(xs) > 1:
+        if unroll:
             for i in range(2 * parts):
                 one(i, 0)
         else:
             lax.fori_loop(0, 2 * parts, one, 0)
 
 
-def partials(tok, xs, gate, up, gm, um, unit, units, hand_on=False):
+def partials(tok, xs, gate, up, gm, um, unit, units, hand_on, unroll):
     rows, depth = xs[0].shape
     out = jax.ShapeDtypeStruct((2, rows * len(xs), units), jnp.bfloat16)
     first = tok is None
     return pl.pallas_call(
-        functools.partial(partial_kernel, depth // gm.shape[0], unit, first, hand_on),
+        functools.partial(partial_kernel, depth // gm.shape[0], unit, first, hand_on, unroll),
         in_specs=[ANY] * (4 if first else 5) + [VMEM] * len(xs),
         out_specs=[VMEM] * (3 if hand_on else 2) + [ANY],
         out_shape=[out, out] + [jax.ShapeDtypeStruct((rows, depth), jnp.bfloat16)] * hand_on + [TOKEN],
@@ -99,7 +99,7 @@
         ],
         input_output_aliases={} if first else {4: 3 if hand_on else 2},
         cost_estimate=LONG,
-        compiler_params=pltpu.CompilerParams(vmem_limit_bytes=48 * MIB),
+        compiler_params=pltpu.CompilerParams(vmem_limit_bytes=(46 if unroll else 48) * MIB),
     )(gm, um, gate, up, *([] if first else [tok]), *xs)
 
 
@@ -312,7 +312,7 @@
         ],
         input_output_aliases=aliases,
         cost_estimate=LONG,
-        compiler_params=pltpu.CompilerParams(vmem_limit_bytes=48 * MIB),
+        compiler_params=pltpu.CompilerParams(vmem_limit_bytes=46 * MIB),
     )(z, mask, tok, down, *[h[3] for h in hidden], *([total] if more else []))
     return res[:-1], res[-1]
 
@@ -348,8 +348,10 @@
 
 
 def pieces(group, n_unit):
-    count = 2 if n_unit % 2 == 0 else 1
-    return [(u, count) for u in range(0, n_unit, count)]
+    if n_unit % 2 or group == [1]:
+        return [(u, 1) for u in range(n_unit)]
+    halves = [(u, 2) for u in range(0, n_unit, 2)]
+    return halves if group == [0] else halves[:-1] + [(n_unit - 2, 1), (n_unit - 1, 1)]
 
 
 def shards(n_row, n_col, tokens, gate, up, down, gm, um, dm):
@@ -387,7 +389,7 @@
     def compute(group, u):
         def run(tok):
             hand_on = group == [0] and u == min(1, n_unit - 1)
-            pa, pb, *passed, tok = partials(tok, [xs[d] for d in group], gate, up, gm, um, u, units, hand_on)
+            pa, pb, *passed, tok = partials(tok, [xs[d] for d in group], gate, up, gm, um, u, units, hand_on, group != [0])
             if hand_on:
                 for d in [*range(2, n_row), 1]:
                     xs[d] = swap(passed[0], d)
@@ -407,7 +409,7 @@
                     for i, side, buf in places(chunks.index((d, u))):
                         hidden.append((i, side * count + u - first, b, buf))
             key, last = tuple(g), first + count == n_unit
-            res, tok = project(tok, z, hidden, down, dm, units, first, count, len(g), totals.get(key), last, g == [1])
+            res, tok = project(tok, z, hidden, down, dm, units, first, count, len(g), totals.get(key), last, g == [1] and last)
             if last:
                 outs.update(zip(g, res))
                 if len(g) > 1:

time: 212 us -> 208 us (0.981)
  waiting for transfers between devices: 29.1 us -> 20 us
  Pallas kernels: 98.8 us -> 104 us
    pallas_call x6 -> x9, Pallas kernels: 33.9 us -> 41 us  [project(): pl.pallas_call(functools.partial(project_kernel, tuple((h[:3] for h in hi...]
    ppermute x18, waiting for transfers between devices: 4.32 us -> 0.05 us  [shards(): right_came[t] = lax.ppermute(right_on[t], ('row', 'col'), to_right)]
  transfers between devices with their start and end apart: 78 -> 78, of which waited for: 18 -> 18; matrix products, arithmetic and copies ran while one was open for 0% -> 0% of each run, Pallas kernels for 44% -> 48%
where the time goes in v1:
time: 208 us; the launch traced here: 207 us
  Pallas kernels  104 us (50%)
  starting transfers between devices  77.7 us (37%)
  waiting for transfers between devices  20 us (10%)
  local copies, waits for them, and re-layouts  3.5 us (2%)
    pallas_call x12, Pallas kernels, partials(): pl.pallas_call(functools.partial(partial_kernel, depth // gm.shape[0], un...  52.9 us
    pallas_call x9, Pallas kernels, project(): pl.pallas_call(functools.partial(project_kernel, tuple((h[:3] for h in hi...  41 us
    ppermute x18, starting transfers between devices, shards(): right_got[t] = lax.ppermute(sums[1], ('row', 'col'), to_right)  34.2 us
    ppermute x18, starting transfers between devices, shards(): right_came[t] = lax.ppermute(right_on[t], ('row', 'col'), to_right)  33.4 us
    ppermute x18, waiting for transfers between devices, shards(): left_got[t] = lax.ppermute(sums[0], ('row', 'col'), to_left)  14.2 us
    pallas_call x18, Pallas kernels, sum_step(): pl.pallas_call(functools.partial(sum_kernel, own, n_col, goes_on, ends),...  7.6 us
    ppermute x18, starting transfers between devices, shards(): left_got[t] = lax.ppermute(sums[0], ('row', 'col'), to_left)  6.44 us
  transfers between devices with their start and end apart: 78, of which 18 were waited for; matrix products, arithmetic and copies ran while one was open for 0% of the time, Pallas kernels for 48%

profile of v1, /device:TPU:0, one launch (start us, length us, event | category | flops | bytes accessed | tf_op | source)
XLA Modules:
  0.0 207.2 jit_solution(4286036333991329656)
XLA Ops:
  2.4 4.5 %shard_map.73 = (bf16[2,128,512]{2,1,0:T(8,128)(2,1)S(1)}, bf16[2,128,512]{2,1,0:T(8,128)(2,1)S(1)}, f32[8,128]{1,0:T(8,128)S(1)}) custom-call(s32[16,32]{1,0:T(8,128)S(1)} %copy-done.4, s32[16,32]{1,0:T(8,128)S(1)} %copy-done.6, bf16[2048,4096]{1,0:T(8,128)(2,1)} %gate.23, bf16[2048,4096]{1,0:T(8,128)(2,1)} %up.23, bf16[128,2048]{1,0:T(8,128)(2,1)S(1)} %copy-done), custom_call_target="tpu_custom_call" | custom-call | flops 6442450944 | bytes 16777216 | tf_op jit(solution)/shard_map/pallas_call | solution.py:89
  7.4 2.6 %collective-permute-start.1 = (bf16[2,128,512]{2,1,0:T(8,128)(2,1)S(1)}, bf16[2,128,512]{2,1,0:T(8,128)(2,1)S(1)}, u32[]{:S(2)}, u32[]{:S(2)}) collective-permute-start(bf16[2,128,512]{2,1,0:T(8,128)(2,1)S(1)} %get-tuple-element.187.rest_3_.rest_5_.rest_7_), channel_id=1, source_target_pairs={{0,1},{1,2},{2,3},{3,7},{7,6},{6,5},{5,4},{4,0},{8,9},{9,10},{10,1... | collective-permute-start | bytes 786440 | tf_op jit(solution)/shard_map/ppermute | solution.py:454
  10.0 5.1 %shard_map.74 = (bf16[2,128,512]{2,1,0:T(8,128)(2,1)S(1)}, bf16[2,128,512]{2,1,0:T(8,128)(2,1)S(1)}, bf16[128,2048]{1,0:T(8,128)(2,1)}, f32[8,128]{1,0:T(8,128)S(1)}) custom-call(s32[16,32]{1,0:T(8,128)S(1)} %copy-done.4, s32[16,32]{1,0:T(8,128)S(1)} %copy-done.6, bf16[2048,4096]{1,0:T(8,128)(2,1)} %gate.23, ...), custom_call_target="tpu_custom_call", output_to_operand_aliasing={{3}: (4, {})} | custom-call | flops 6442450944 | bytes 16777216 | tf_op jit(solution)/shard_map/pallas_call | solution.py:89
  19.3 4.5 %shard_map.76 = (bf16[2,128,512]{2,1,0:T(8,128)(2,1)S(1)}, bf16[2,128,512]{2,1,0:T(8,128)(2,1)S(1)}, f32[8,128]{1,0:T(8,128)S(1)}) custom-call(s32[16,32]{1,0:T(8,128)S(1)} %copy-done.5, s32[16,32]{1,0:T(8,128)S(1)} %copy-done.7, bf16[2048,4096]{1,0:T(8,128)(2,1)} %gate.23, bf16[2048,4096]{1,0:T(8,128)(2,1)} %up.23, ...), custom_call_target="tpu_custom_call", output_to_operand_aliasing={{2}: (4, {})} | custom-call | flops 6442450944 | bytes 16777216 | tf_op jit(solution)/shard_map/pallas_call | solution.py:89
  28.2 4.5 %shard_map.78 = (bf16[2,128,512]{2,1,0:T(8,128)(2,1)S(1)}, bf16[2,128,512]{2,1,0:T(8,128)(2,1)S(1)}, f32[8,128]{1,0:T(8,128)S(1)}) custom-call(s32[16,32]{1,0:T(8,128)S(1)} %copy-done.5, s32[16,32]{1,0:T(8,128)S(1)} %copy-done.7, bf16[2048,4096]{1,0:T(8,128)(2,1)} %gate.23, bf16[2048,4096]{1,0:T(8,128)(2,1)} %up.23, ...), custom_call_target="tpu_custom_call", output_to_operand_aliasing={{2}: (4, {})} | custom-call | flops 6442450944 | bytes 16777216 | tf_op jit(solution)/shard_map/pallas_call | solution.py:89
  39.6 4.6 %shard_map.81 = (bf16[2,256,512]{2,1,0:T(8,128)(2,1)S(1)}, bf16[2,256,512]{2,1,0:T(8,128)(2,1)S(1)}, f32[8,128]{1,0:T(8,128)S(1)}) custom-call(s32[16,32]{1,0:T(8,128)S(1)} %copy-done.5, s32[16,32]{1,0:T(8,128)S(1)} %copy-done.7, bf16[2048,4096]{1,0:T(8,128)(2,1)} %gate.23, bf16[2048,4096]{1,0:T(8,128)(2,1)} %up.23, ...), custom_call_target="tpu_custom_call", output_to_operand_aliasing={{2}: (4, {})} | custom-call | flops 6442450944 | bytes 16777216 | tf_op jit(solution)/shard_map/pallas_call | solution.py:89
  50.7 4.2 %collective-permute-done.12.left_in = bf16[2,128,512]{2,1,0:T(8,128)(2,1)} collective-permute-done((bf16[2,128,512]{2,1,0:T(8,128)(2,1)}, bf16[2,128,512]{2,1,0:T(8,128)(2,1)}, u32[]{:S(2)}, u32[]{:S(2)}) %collective-permute-start.12) | collective-permute-done | bytes 262176 | tf_op jit(solution)/shard_map/ppermute | solution.py:453
  60.8 2.0 collective-permute-start.18
  62.8 4.6 %shard_map.86 = (bf16[2,256,512]{2,1,0:T(8,128)(2,1)S(1)}, bf16[2,256,512]{2,1,0:T(8,128)(2,1)S(1)}, f32[8,128]{1,0:T(8,128)S(1)}) custom-call(s32[16,32]{1,0:T(8,128)S(1)} %copy-done.5, s32[16,32]{1,0:T(8,128)S(1)} %copy-done.7, bf16[2048,4096]{1,0:T(8,128)(2,1)} %gate.23, bf16[2048,4096]{1,0:T(8,128)(2,1)} %up.23, ...), custom_call_target="tpu_custom_call", output_to_operand_aliasing={{2}: (4, {})} | custom-call | flops 6442450944 | bytes 16777216 | tf_op jit(solution)/shard_map/pallas_call | solution.py:89
  72.0 4.6 %shard_map.89 = (bf16[2,256,512]{2,1,0:T(8,128)(2,1)S(1)}, bf16[2,256,512]{2,1,0:T(8,128)(2,1)S(1)}, f32[8,128]{1,0:T(8,128)S(1)}) custom-call(s32[16,32]{1,0:T(8,128)S(1)} %copy-done.5, s32[16,32]{1,0:T(8,128)S(1)} %copy-done.7, bf16[2048,4096]{1,0:T(8,128)(2,1)} %gate.23, bf16[2048,4096]{1,0:T(8,128)(2,1)} %up.23, ...), custom_call_target="tpu_custom_call", output_to_operand_aliasing={{2}: (4, {})} | custom-call | flops 6442450944 | bytes 16777216 | tf_op jit(solution)/shard_map/pallas_call | solution.py:89
  81.4 6.4 %shard_map.92 = (f32[128,2048]{1,0:T(8,128)S(1)}, f32[8,128]{1,0:T(8,128)S(1)}) custom-call(s32[1]{0:T(128)} %bitcast.z_ref, s32[32,16]{1,0:T(8,128)S(1)} %copy.69.mask, f32[8,128]{1,0:T(8,128)S(1)} %get-tuple-element.240.tok, bf16[4096,2048]{1,0:T(8,128)(2,1)} %down.17, bf16[128,512]{1,0:T(8,128)(2,1)S(1)} %copy-done.11, ...), custom_call_target="tpu_custom_call", output_to_operand_aliasing={{1}: (2, {})} | custom-call | flops 6442450944 | bytes 16777216 | tf_op jit(solution)/shard_map/pallas_call | solution.py:302
  92.1 4.6 %shard_map.95 = (bf16[2,256,512]{2,1,0:T(8,128)(2,1)S(1)}, bf16[2,256,512]{2,1,0:T(8,128)(2,1)S(1)}, f32[8,128]{1,0:T(8,128)S(1)}) custom-call(s32[16,32]{1,0:T(8,128)S(1)} %copy-done.5, s32[16,32]{1,0:T(8,128)S(1)} %copy-done.7, bf16[2048,4096]{1,0:T(8,128)(2,1)} %gate.23, bf16[2048,4096]{1,0:T(8,128)(2,1)} %up.23, ...), custom_call_target="tpu_custom_call", output_to_operand_aliasing={{2}: (4, {})} | custom-call | flops 6442450944 | bytes 16777216 | tf_op jit(solution)/shard_map/pallas_call | solution.py:89
  101.2 5.3 %shard_map.98 = (bf16[128,2048]{1,0:T(8,128)(2,1)S(1)}, f32[8,128]{1,0:T(8,128)S(1)}) custom-call(s32[1]{0:T(128)} %bitcast.z_ref, s32[32,16]{1,0:T(8,128)S(1)} %copy.69.mask, f32[8,128]{1,0:T(8,128)S(1)} %get-tuple-element.258.tok, bf16[4096,2048]{1,0:T(8,128)(2,1)} %down.17, ...), custom_call_target="tpu_custom_call", output_to_operand_aliasing={{1}: (2, {})} | custom-call | flops 6442450944 | bytes 16777216 | tf_op jit(solution)/shard_map/pallas_call | solution.py:302
  110.9 4.0 %shard_map.101 = (bf16[2,128,512]{2,1,0:T(8,128)(2,1)S(1)}, bf16[2,128,512]{2,1,0:T(8,128)(2,1)S(1)}, f32[8,128]{1,0:T(8,128)S(1)}) custom-call(s32[16,32]{1,0:T(8,128)S(1)} %copy-done.5, s32[16,32]{1,0:T(8,128)S(1)} %copy-done.7, bf16[2048,4096]{1,0:T(8,128)(2,1)} %gate.23, bf16[2048,4096]{1,0:T(8,128)(2,1)} %up.23, ...), custom_call_target="tpu_custom_call", output_to_operand_aliasing={{2}: (4, {})} | custom-call | flops 6442450944 | bytes 16777216 | tf_op jit(solution)/shard_map/pallas_call | solution.py:89
  119.5 4.0 %shard_map.104 = (bf16[2,128,512]{2,1,0:T(8,128)(2,1)S(1)}, bf16[2,128,512]{2,1,0:T(8,128)(2,1)S(1)}, f32[8,128]{1,0:T(8,128)S(1)}) custom-call(s32[16,32]{1,0:T(8,128)S(1)} %copy-done.5, s32[16,32]{1,0:T(8,128)S(1)} %copy-done.7, bf16[2048,4096]{1,0:T(8,128)(2,1)} %gate.23, bf16[2048,4096]{1,0:T(8,128)(2,1)} %up.23, ...), custom_call_target="tpu_custom_call", output_to_operand_aliasing={{2}: (4, {})} | custom-call | flops 6442450944 | bytes 16777216 | tf_op jit(solution)/shard_map/pallas_call | solution.py:89
  128.8 4.0 %shard_map.107 = (bf16[2,128,512]{2,1,0:T(8,128)(2,1)S(1)}, bf16[2,128,512]{2,1,0:T(8,128)(2,1)S(1)}, f32[8,128]{1,0:T(8,128)S(1)}) custom-call(s32[16,32]{1,0:T(8,128)S(1)} %copy-done.5, s32[16,32]{1,0:T(8,128)S(1)} %copy-done.7, bf16[2048,4096]{1,0:T(8,128)(2,1)} %gate.23, bf16[2048,4096]{1,0:T(8,128)(2,1)} %up.23, ...), custom_call_target="tpu_custom_call", output_to_operand_aliasing={{2}: (4, {})} | custom-call | flops 6442450944 | bytes 16777216 | tf_op jit(solution)/shard_map/pallas_call | solution.py:89
  133.4 2.0 collective-permute-start.50
  137.3 6.0 %shard_map.110 = (f32[256,2048]{1,0:T(8,128)S(1)}, f32[8,128]{1,0:T(8,128)S(1)}) custom-call(s32[1]{0:T(128)} %bitcast.z_ref, s32[32,16]{1,0:T(8,128)S(1)} %copy.69.mask, f32[8,128]{1,0:T(8,128)S(1)} %get-tuple-element.298.tok, bf16[4096,2048]{1,0:T(8,128)(2,1)} %down.17, ...), custom_call_target="tpu_custom_call", output_to_operand_aliasing={{1}: (2, {})} | custom-call | flops 6442450944 | bytes 16777216 | tf_op jit(solution)/shard_map/pallas_call | solution.py:302
  143.7 2.0 collective-permute-start.54
  147.8 4.0 %shard_map.113 = (bf16[2,128,512]{2,1,0:T(8,128)(2,1)S(1)}, bf16[2,128,512]{2,1,0:T(8,128)(2,1)S(1)}, f32[8,128]{1,0:T(8,128)S(1)}) custom-call(s32[16,32]{1,0:T(8,128)S(1)} %copy-done.5, s32[16,32]{1,0:T(8,128)S(1)} %copy-done.7, bf16[2048,4096]{1,0:T(8,128)(2,1)} %gate.23, bf16[2048,4096]{1,0:T(8,128)(2,1)} %up.23, ...), custom_call_target="tpu_custom_call", output_to_operand_aliasing={{2}: (4, {})} | custom-call | flops 6442450944 | bytes 16777216 | tf_op jit(solution)/shard_map/pallas_call | solution.py:89
  152.5 2.0 collective-permute-start.58
  156.3 4.3 %shard_map.116 = (f32[256,2048]{1,0:T(8,128)S(1)}, f32[8,128]{1,0:T(8,128)S(1)}) custom-call(s32[1]{0:T(128)} %bitcast.z_ref, s32[32,16]{1,0:T(8,128)S(1)} %copy.69.mask, f32[8,128]{1,0:T(8,128)S(1)} %get-tuple-element.318.tok, bf16[4096,2048]{1,0:T(8,128)(2,1)} %down.17, ...), custom_call_target="tpu_custom_call", output_to_operand_aliasing={{1}: (2, {}), {0}: (20, {})} | custom-call | flops 6442450944 | bytes 16777216 | tf_op jit(solution)/shard_map/pallas_call | solution.py:302
  161.0 2.0 collective-permute-start.62
  165.0 4.4 %collective-permute-done.61.left_in = bf16[2,128,512]{2,1,0:T(8,128)(2,1)S(1)} collective-permute-done((bf16[2,128,512]{2,1,0:T(8,128)(2,1)S(1)}, bf16[2,128,512]{2,1,0:T(8,128)(2,1)S(1)}, u32[]{:S(2)}, u32[]{:S(2)}) %collective-permute-start.61) | collective-permute-done | bytes 262176 | tf_op jit(solution)/shard_map/ppermute | solution.py:453
  169.9 2.4 %collective-permute-start.66 = (bf16[2,128,512]{2,1,0:T(8,128)(2,1)S(1)}, bf16[2,128,512]{2,1,0:T(8,128)(2,1)S(1)}, u32[]{:S(2)}, u32[]{:S(2)}) collective-permute-start(bf16[2,128,512]{2,1,0:T(8,128)(2,1)S(1)} %get-tuple-element.340), channel_id=1, source_target_pairs={{0,1},{1,2},{2,3},{3,7},{7,6},{6,5},{5,4},{4,0},{8,9},{9,10},{10,1... | collective-permute-start | bytes 786440 | tf_op jit(solution)/shard_map/ppermute | solution.py:454
  172.4 2.5 %collective-permute-start.67 = (bf16[128,512]{1,0:T(8,128)(2,1)S(1)}, bf16[128,512]{1,0:T(8,128)(2,1)S(1)}, u32[]{:S(2)}, u32[]{:S(2)}) collective-permute-start(bf16[128,512]{1,0:T(8,128)(2,1)S(1)} %get-tuple-element.335.rest_14_.rest_4_.rest_2_.rest_0_), channel_id=1, source_target_pairs={{0,1},{1,2},{2,3},{3,7},{7,6},{6,5},{5,4},{4,0},{8,9},{9,10},{10,1... | collective-permute-start | bytes 393224 | tf_op jit(solution)/shard_map/ppermute | solution.py:459
  174.9 4.3 %shard_map.121 = (bf16[128,2048]{1,0:T(8,128)(2,1)S(1)}, bf16[128,2048]{1,0:T(8,128)(2,1)S(1)}, f32[8,128]{1,0:T(8,128)S(1)}) custom-call(s32[1]{0:T(128)} %bitcast.z_ref, s32[32,16]{1,0:T(8,128)S(1)} %copy.69.mask, f32[8,128]{1,0:T(8,128)S(1)} %get-tuple-element.334.tok, bf16[4096,2048]{1,0:T(8,128)(2,1)} %down.17, ...), custom_call_target="tpu_custom_call", output_to_operand_aliasing={{2}: (2, {})} | custom-call | flops 6442450944 | bytes 16777216 | tf_op jit(solution)/shard_map/pallas_call | solution.py:302
  181.6 3.8 %shard_map.125 = (f32[128,2048]{1,0:T(8,128)S(1)}, f32[8,128]{1,0:T(8,128)S(1)}) custom-call(s32[1]{0:T(128)} %bitcast.z_ref, s32[32,16]{1,0:T(8,128)S(1)} %copy.69.mask, f32[8,128]{1,0:T(8,128)S(1)} %get-tuple-element.347.tok, bf16[4096,2048]{1,0:T(8,128)(2,1)} %down.17, ...), custom_call_target="tpu_custom_call", output_to_operand_aliasing={{1}: (2, {})} | custom-call | flops 6442450944 | bytes 16777216 | tf_op jit(solution)/shard_map/pallas_call | solution.py:302
  189.8 3.8 %shard_map.127 = (f32[128,2048]{1,0:T(8,128)S(1)}, f32[8,128]{1,0:T(8,128)S(1)}) custom-call(s32[1]{0:T(128)} %bitcast.z_ref, s32[32,16]{1,0:T(8,128)S(1)} %copy.69.mask, f32[8,128]{1,0:T(8,128)S(1)} %get-tuple-element.351.tok, bf16[4096,2048]{1,0:T(8,128)(2,1)} %down.17, ...), custom_call_target="tpu_custom_call", output_to_operand_aliasing={{1}: (2, {}), {0}: (12, {})} | custom-call | flops 6442450944 | bytes 16777216 | tf_op jit(solution)/shard_map/pallas_call | solution.py:302
  193.7 2.0 collective-permute-start.75
  195.7 3.8 %shard_map.129 = (f32[128,2048]{1,0:T(8,128)S(1)}, f32[8,128]{1,0:T(8,128)S(1)}) custom-call(s32[1]{0:T(128)} %bitcast.z_ref, s32[32,16]{1,0:T(8,128)S(1)} %copy.69.mask, f32[8,128]{1,0:T(8,128)S(1)} %get-tuple-element.356.tok, bf16[4096,2048]{1,0:T(8,128)(2,1)} %down.17, ...), custom_call_target="tpu_custom_call", output_to_operand_aliasing={{1}: (2, {}), {0}: (12, {})} | custom-call | flops 6442450944 | bytes 16777216 | tf_op jit(solution)/shard_map/pallas_call | solution.py:302
  200.7 3.5 %shard_map.130 = (bf16[128,2048]{1,0:T(8,128)(2,1)S(1)}, f32[8,128]{1,0:T(8,128)S(1)}) custom-call(s32[1]{0:T(128)} %bitcast.z_ref, s32[32,16]{1,0:T(8,128)S(1)} %copy.69.mask, f32[8,128]{1,0:T(8,128)S(1)} %get-tuple-element.360.tok, bf16[4096,2048]{1,0:T(8,128)(2,1)} %down.17, ...), custom_call_target="tpu_custom_call", output_to_operand_aliasing={{1}: (2, {})} | custom-call | flops 6442450944 | bytes 16777216 | tf_op jit(solution)/shard_map/pallas_call | solution.py:302
  (210 shorter events, 84.2 us)
Async XLA Ops:
  6.9 10.2 %collective-permute-start = (bf16[2,128,512]{2,1,0:T(8,128)(2,1)S(1)}, bf16[2,128,512]{2,1,0:T(8,128)(2,1)S(1)}, u32[]{:S(2)}, u32[]{:S(2)}) collective-permute-start(bf16[2,128,512]{2,1,0:T(8,128)(2,1)S(1)} %get-tuple-element.186.rest_0_), channel_id=1, source_target_pairs={{1,0},{2,1},{3,2},{7,3},{6,7},{5,6},{4,5},{0,4},{9,8},{10,9},{11,1... | collective-permute-start | bytes 786440 | tf_op jit(solution)/shard_map/ppermute | solution.py:453
  7.4 9.8 %collective-permute-start.1 = (bf16[2,128,512]{2,1,0:T(8,128)(2,1)S(1)}, bf16[2,128,512]{2,1,0:T(8,128)(2,1)S(1)}, u32[]{:S(2)}, u32[]{:S(2)}) collective-permute-start(bf16[2,128,512]{2,1,0:T(8,128)(2,1)S(1)} %get-tuple-element.187.rest_3_.rest_5_.rest_7_), channel_id=1, source_target_pairs={{0,1},{1,2},{2,3},{3,7},{7,6},{6,5},{5,4},{4,0},{8,9},{9,10},{10,1... | collective-permute-start | bytes 786440 | tf_op jit(solution)/shard_map/ppermute | solution.py:454
  15.1 24.5 %collective-permute-start.6 = (bf16[128,2048]{1,0:T(8,128)(2,1)}, bf16[128,2048]{1,0:T(8,128)(2,1)S(1)}, u32[]{:S(2)}, u32[]{:S(2)}) collective-permute-start(bf16[128,2048]{1,0:T(8,128)(2,1)} %get-tuple-element.205), channel_id=1, source_target_pairs={{8,0},{12,4},{0,8},{4,12},{9,1},{13,5},{1,9},{5,13},{10,2},{14,6},... | collective-permute-start | bytes 1572872 | tf_op jit(solution)/shard_map/ppermute | solution.py:370
  17.1 22.5 %collective-permute-start.7 = (bf16[128,2048]{1,0:T(8,128)(2,1)}, bf16[128,2048]{1,0:T(8,128)(2,1)S(1)}, u32[]{:S(2)}, u32[]{:S(2)}) collective-permute-start(bf16[128,2048]{1,0:T(8,128)(2,1)} %get-tuple-element.205), channel_id=1, source_target_pairs={{12,0},{8,4},{4,8},{0,12},{13,1},{9,5},{5,9},{1,13},{14,2},{10,6},... | collective-permute-start | bytes 1572872 | tf_op jit(solution)/shard_map/ppermute | solution.py:370
  35.0 9.3 %collective-permute-start.8 = (bf16[2,128,512]{2,1,0:T(8,128)(2,1)S(1)}, bf16[2,128,512]{2,1,0:T(8,128)(2,1)S(1)}, u32[]{:S(2)}, u32[]{:S(2)}) collective-permute-start(bf16[2,128,512]{2,1,0:T(8,128)(2,1)S(1)} %get-tuple-element.207), channel_id=1, source_target_pairs={{1,0},{2,1},{3,2},{7,3},{6,7},{5,6},{4,5},{0,4},{9,8},{10,9},{11,1... | collective-permute-start | bytes 786440 | tf_op jit(solution)/shard_map/ppermute | solution.py:453
  37.7 10.3 %collective-permute-start.10 = (bf16[128,512]{1,0:T(8,128)(2,1)S(1)}, bf16[128,512]{1,0:T(8,128)(2,1)S(1)}, u32[]{:S(2)}, u32[]{:S(2)}) collective-permute-start(bf16[128,512]{1,0:T(8,128)(2,1)S(1)} %get-tuple-element.213.rest_0_), channel_id=1, source_target_pairs={{0,1},{1,2},{2,3},{3,7},{7,6},{6,5},{5,4},{4,0},{8,9},{9,10},{10,1... | collective-permute-start | bytes 393224 | tf_op jit(solution)/shard_map/ppermute | solution.py:459
  45.5 9.5 %collective-permute-start.12 = (bf16[2,128,512]{2,1,0:T(8,128)(2,1)}, bf16[2,128,512]{2,1,0:T(8,128)(2,1)}, u32[]{:S(2)}, u32[]{:S(2)}) collective-permute-start(bf16[2,128,512]{2,1,0:T(8,128)(2,1)} %get-tuple-element.216), channel_id=1, source_target_pairs={{1,0},{2,1},{3,2},{7,3},{6,7},{5,6},{4,5},{0,4},{9,8},{10,9},{11,1... | collective-permute-start | bytes 786440 | tf_op jit(solution)/shard_map/ppermute | solution.py:453
  48.7 11.1 %collective-permute-start.14 = (bf16[128,512]{1,0:T(8,128)(2,1)}, bf16[128,512]{1,0:T(8,128)(2,1)}, u32[]{:S(2)}, u32[]{:S(2)}) collective-permute-start(bf16[128,512]{1,0:T(8,128)(2,1)} %get-tuple-element.220.rest_2_.rest_8_), channel_id=1, source_target_pairs={{0,1},{1,2},{2,3},{3,7},{7,6},{6,5},{5,4},{4,0},{8,9},{9,10},{10,1... | collective-permute-start | bytes 393224 | tf_op jit(solution)/shard_map/ppermute | solution.py:459
  50.7 9.1 %collective-permute-start.15 = (bf16[128,512]{1,0:T(8,128)(2,1)}, bf16[128,512]{1,0:T(8,128)(2,1)}, u32[]{:S(2)}, u32[]{:S(2)}) collective-permute-start(bf16[128,512]{1,0:T(8,128)(2,1)} %get-tuple-element.221.rest_3_.rest_9_), channel_id=1, source_target_pairs={{1,0},{2,1},{3,2},{7,3},{6,7},{5,6},{4,5},{0,4},{9,8},{10,9},{11,1... | collective-permute-start | bytes 393224 | tf_op jit(solution)/shard_map/ppermute | solution.py:458
  50.7 60.3 %collective-permute-start.36 = (bf16[128,2048]{1,0:T(8,128)(2,1)}, bf16[128,2048]{1,0:T(8,128)(2,1)S(1)}, u32[]{:S(2)}, u32[]{:S(2)}) collective-permute-start(bf16[128,2048]{1,0:T(8,128)(2,1)} %get-tuple-element.205), channel_id=1, source_target_pairs={{4,0},{0,4},{12,8},{8,12},{5,1},{1,5},{13,9},{9,13},{6,2},{2,6},{1... | collective-permute-start | bytes 1572872 | tf_op jit(solution)/shard_map/ppermute | solution.py:370
  57.3 10.1 %collective-permute-start.16 = (bf16[2,128,512]{2,1,0:T(8,128)(2,1)S(1)}, bf16[2,128,512]{2,1,0:T(8,128)(2,1)S(1)}, u32[]{:S(2)}, u32[]{:S(2)}) collective-permute-start(bf16[2,128,512]{2,1,0:T(8,128)(2,1)S(1)} %get-tuple-element.224), channel_id=1, source_target_pairs={{1,0},{2,1},{3,2},{7,3},{6,7},{5,6},{4,5},{0,4},{9,8},{10,9},{11,1... | collective-permute-start | bytes 786440 | tf_op jit(solution)/shard_map/ppermute | solution.py:453
  58.3 9.1 %collective-permute-start.17 = (bf16[2,128,512]{2,1,0:T(8,128)(2,1)S(1)}, bf16[2,128,512]{2,1,0:T(8,128)(2,1)S(1)}, u32[]{:S(2)}, u32[]{:S(2)}) collective-permute-start(bf16[2,128,512]{2,1,0:T(8,128)(2,1)S(1)} %get-tuple-element.225), channel_id=1, source_target_pairs={{0,1},{1,2},{2,3},{3,7},{7,6},{6,5},{5,4},{4,0},{8,9},{9,10},{10,1... | collective-permute-start | bytes 786440 | tf_op jit(solution)/shard_map/ppermute | solution.py:454
  60.8 9.0 %collective-permute-start.18 = (bf16[128,512]{1,0:T(8,128)(2,1)S(1)}, bf16[128,512]{1,0:T(8,128)(2,1)S(1)}, u32[]{:S(2)}, u32[]{:S(2)}) collective-permute-start(bf16[128,512]{1,0:T(8,128)(2,1)S(1)} %get-tuple-element.230.rest_4_.rest_10_.rest_0_), channel_id=1, source_target_pairs={{0,1},{1,2},{2,3},{3,7},{7,6},{6,5},{5,4},{4,0},{8,9},{9,10},{10,1... | collective-permute-start | bytes 393224 | tf_op jit(solution)/shard_map/ppermute | solution.py:459
  70.0 9.3 %collective-permute-start.22 = (bf16[128,512]{1,0:T(8,128)(2,1)S(1)}, bf16[128,512]{1,0:T(8,128)(2,1)S(1)}, u32[]{:S(2)}, u32[]{:S(2)}) collective-permute-start(bf16[128,512]{1,0:T(8,128)(2,1)S(1)} %get-tuple-element.238.rest_6_.rest_12_.rest_2_.rest_8_), channel_id=1, source_target_pairs={{0,1},{1,2},{2,3},{3,7},{7,6},{6,5},{5,4},{4,0},{8,9},{9,10},{10,1... | collective-permute-start | bytes 393224 | tf_op jit(solution)/shard_map/ppermute | solution.py:459
  77.0 10.8 %collective-permute-start.24 = (bf16[2,128,512]{2,1,0:T(8,128)(2,1)S(1)}, bf16[2,128,512]{2,1,0:T(8,128)(2,1)S(1)}, u32[]{:S(2)}, u32[]{:S(2)}) collective-permute-start(bf16[2,128,512]{2,1,0:T(8,128)(2,1)S(1)} %get-tuple-element.244), channel_id=1, source_target_pairs={{1,0},{2,1},{3,2},{7,3},{6,7},{5,6},{4,5},{0,4},{9,8},{10,9},{11,1... | collective-permute-start | bytes 786440 | tf_op jit(solution)/shard_map/ppermute | solution.py:453
  78.1 9.6 %collective-permute-start.25 = (bf16[2,128,512]{2,1,0:T(8,128)(2,1)S(1)}, bf16[2,128,512]{2,1,0:T(8,128)(2,1)S(1)}, u32[]{:S(2)}, u32[]{:S(2)}) collective-permute-start(bf16[2,128,512]{2,1,0:T(8,128)(2,1)S(1)} %get-tuple-element.245), channel_id=1, source_target_pairs={{0,1},{1,2},{2,3},{3,7},{7,6},{6,5},{5,4},{4,0},{8,9},{9,10},{10,1... | collective-permute-start | bytes 786440 | tf_op jit(solution)/shard_map/ppermute | solution.py:454
  79.4 10.8 %collective-permute-start.26 = (bf16[128,512]{1,0:T(8,128)(2,1)S(1)}, bf16[128,512]{1,0:T(8,128)(2,1)S(1)}, u32[]{:S(2)}, u32[]{:S(2)}) collective-permute-start(bf16[128,512]{1,0:T(8,128)(2,1)S(1)} %get-tuple-element.241.rest_14_.rest_4_.rest_10_.rest_0_), channel_id=1, source_target_pairs={{0,1},{1,2},{2,3},{3,7},{7,6},{6,5},{5,4},{4,0},{8,9},{9,10},{10,1... | collective-permute-start | bytes 393224 | tf_op jit(solution)/shard_map/ppermute | solution.py:459
  88.2 9.1 %collective-permute-start.28 = (bf16[2,128,512]{2,1,0:T(8,128)(2,1)S(1)}, bf16[2,128,512]{2,1,0:T(8,128)(2,1)S(1)}, u32[]{:S(2)}, u32[]{:S(2)}) collective-permute-start(bf16[2,128,512]{2,1,0:T(8,128)(2,1)S(1)} %get-tuple-element.252), channel_id=1, source_target_pairs={{1,0},{2,1},{3,2},{7,3},{6,7},{5,6},{4,5},{0,4},{9,8},{10,9},{11,1... | collective-permute-start | bytes 786440 | tf_op jit(solution)/shard_map/ppermute | solution.py:453
  88.2 9.1 %collective-permute-start.29 = (bf16[2,128,512]{2,1,0:T(8,128)(2,1)S(1)}, bf16[2,128,512]{2,1,0:T(8,128)(2,1)S(1)}, u32[]{:S(2)}, u32[]{:S(2)}) collective-permute-start(bf16[2,128,512]{2,1,0:T(8,128)(2,1)S(1)} %get-tuple-element.253), channel_id=1, source_target_pairs={{0,1},{1,2},{2,3},{3,7},{7,6},{6,5},{5,4},{4,0},{8,9},{9,10},{10,1... | collective-permute-start | bytes 786440 | tf_op jit(solution)/shard_map/ppermute | solution.py:454
  90.3 9.5 %collective-permute-start.30 = (bf16[128,512]{1,0:T(8,128)(2,1)S(1)}, bf16[128,512]{1,0:T(8,128)(2,1)S(1)}, u32[]{:S(2)}, u32[]{:S(2)}) collective-permute-start(bf16[128,512]{1,0:T(8,128)(2,1)S(1)} %get-tuple-element.256.rest_6_.rest_12_.rest_2_.rest_16_), channel_id=1, source_target_pairs={{0,1},{1,2},{2,3},{3,7},{7,6},{6,5},{5,4},{4,0},{8,9},{9,10},{10,1... | collective-permute-start | bytes 393224 | tf_op jit(solution)/shard_map/ppermute | solution.py:459
  97.7 8.9 %collective-permute-start.32 = (bf16[2,128,512]{2,1,0:T(8,128)(2,1)S(1)}, bf16[2,128,512]{2,1,0:T(8,128)(2,1)S(1)}, u32[]{:S(2)}, u32[]{:S(2)}) collective-permute-start(bf16[2,128,512]{2,1,0:T(8,128)(2,1)S(1)} %get-tuple-element.264), channel_id=1, source_target_pairs={{1,0},{2,1},{3,2},{7,3},{6,7},{5,6},{4,5},{0,4},{9,8},{10,9},{11,1... | collective-permute-start | bytes 786440 | tf_op jit(solution)/shard_map/ppermute | solution.py:453
  99.8 9.2 %collective-permute-start.34 = (bf16[128,512]{1,0:T(8,128)(2,1)S(1)}, bf16[128,512]{1,0:T(8,128)(2,1)S(1)}, u32[]{:S(2)}, u32[]{:S(2)}) collective-permute-start(bf16[128,512]{1,0:T(8,128)(2,1)S(1)} %get-tuple-element.259.rest_14_.rest_4_.rest_8_.rest_18_), channel_id=1, source_target_pairs={{0,1},{1,2},{2,3},{3,7},{7,6},{6,5},{5,4},{4,0},{8,9},{9,10},{10,1... | collective-permute-start | bytes 393224 | tf_op jit(solution)/shard_map/ppermute | solution.py:459
  106.9 9.0 %collective-permute-start.37 = (bf16[2,128,512]{2,1,0:T(8,128)(2,1)S(1)}, bf16[2,128,512]{2,1,0:T(8,128)(2,1)S(1)}, u32[]{:S(2)}, u32[]{:S(2)}) collective-permute-start(bf16[2,128,512]{2,1,0:T(8,128)(2,1)S(1)} %get-tuple-element.272), channel_id=1, source_target_pairs={{1,0},{2,1},{3,2},{7,3},{6,7},{5,6},{4,5},{0,4},{9,8},{10,9},{11,1... | collective-permute-start | bytes 786440 | tf_op jit(solution)/shard_map/ppermute | solution.py:453
  106.9 9.0 %collective-permute-start.38 = (bf16[2,128,512]{2,1,0:T(8,128)(2,1)S(1)}, bf16[2,128,512]{2,1,0:T(8,128)(2,1)S(1)}, u32[]{:S(2)}, u32[]{:S(2)}) collective-permute-start(bf16[2,128,512]{2,1,0:T(8,128)(2,1)S(1)} %get-tuple-element.273), channel_id=1, source_target_pairs={{0,1},{1,2},{2,3},{3,7},{7,6},{6,5},{5,4},{4,0},{8,9},{9,10},{10,1... | collective-permute-start | bytes 786440 | tf_op jit(solution)/shard_map/ppermute | solution.py:454
  109.0 9.3 %collective-permute-start.39 = (bf16[128,512]{1,0:T(8,128)(2,1)S(1)}, bf16[128,512]{1,0:T(8,128)(2,1)S(1)}, u32[]{:S(2)}, u32[]{:S(2)}) collective-permute-start(bf16[128,512]{1,0:T(8,128)(2,1)S(1)} %get-tuple-element.276.rest_6_.rest_10_.rest_20_.rest_24_), channel_id=1, source_target_pairs={{0,1},{1,2},{2,3},{3,7},{7,6},{6,5},{5,4},{4,0},{8,9},{9,10},{10,1... | collective-permute-start | bytes 393224 | tf_op jit(solution)/shard_map/ppermute | solution.py:459
  133.4 9.9 %collective-permute-start.49 = (bf16[2,128,512]{2,1,0:T(8,128)(2,1)S(1)}, bf16[2,128,512]{2,1,0:T(8,128)(2,1)S(1)}, u32[]{:S(2)}, u32[]{:S(2)}) collective-permute-start(bf16[2,128,512]{2,1,0:T(8,128)(2,1)S(1)} %get-tuple-element.302), channel_id=1, source_target_pairs={{1,0},{2,1},{3,2},{7,3},{6,7},{5,6},{4,5},{0,4},{9,8},{10,9},{11,1... | collective-permute-start | bytes 786440 | tf_op jit(solution)/shard_map/ppermute | solution.py:453
  133.4 9.9 %collective-permute-start.50 = (bf16[2,128,512]{2,1,0:T(8,128)(2,1)S(1)}, bf16[2,128,512]{2,1,0:T(8,128)(2,1)S(1)}, u32[]{:S(2)}, u32[]{:S(2)}) collective-permute-start(bf16[2,128,512]{2,1,0:T(8,128)(2,1)S(1)} %get-tuple-element.303), channel_id=1, source_target_pairs={{0,1},{1,2},{2,3},{3,7},{7,6},{6,5},{5,4},{4,0},{8,9},{9,10},{10,1... | collective-permute-start | bytes 786440 | tf_op jit(solution)/shard_map/ppermute | solution.py:454
  135.5 10.3 %collective-permute-start.51 = (bf16[128,512]{1,0:T(8,128)(2,1)S(1)}, bf16[128,512]{1,0:T(8,128)(2,1)S(1)}, u32[]{:S(2)}, u32[]{:S(2)}) collective-permute-start(bf16[128,512]{1,0:T(8,128)(2,1)S(1)} %get-tuple-element.299.rest_30_.rest_4_.rest_10_.rest_0_), channel_id=1, source_target_pairs={{0,1},{1,2},{2,3},{3,7},{7,6},{6,5},{5,4},{4,0},{8,9},{9,10},{10,1... | collective-permute-start | bytes 393224 | tf_op jit(solution)/shard_map/ppermute | solution.py:459
  163.0 9.3 %collective-permute-start.63 = (bf16[128,512]{1,0:T(8,128)(2,1)S(1)}, bf16[128,512]{1,0:T(8,128)(2,1)S(1)}, u32[]{:S(2)}, u32[]{:S(2)}) collective-permute-start(bf16[128,512]{1,0:T(8,128)(2,1)S(1)} %get-tuple-element.332.rest_6_.rest_12_.rest_2_.rest_0_), channel_id=1, source_target_pairs={{0,1},{1,2},{2,3},{3,7},{7,6},{6,5},{5,4},{4,0},{8,9},{9,10},{10,1... | collective-permute-start | bytes 393224 | tf_op jit(solution)/shard_map/ppermute | solution.py:459
  169.9 9.4 %collective-permute-start.65 = (bf16[2,128,512]{2,1,0:T(8,128)(2,1)S(1)}, bf16[2,128,512]{2,1,0:T(8,128)(2,1)S(1)}, u32[]{:S(2)}, u32[]{:S(2)}) collective-permute-start(bf16[2,128,512]{2,1,0:T(8,128)(2,1)S(1)} %get-tuple-element.339), channel_id=1, source_target_pairs={{1,0},{2,1},{3,2},{7,3},{6,7},{5,6},{4,5},{0,4},{9,8},{10,9},{11,1... | collective-permute-start | bytes 786440 | tf_op jit(solution)/shard_map/ppermute | solution.py:453
  169.9 9.3 %collective-permute-start.66 = (bf16[2,128,512]{2,1,0:T(8,128)(2,1)S(1)}, bf16[2,128,512]{2,1,0:T(8,128)(2,1)S(1)}, u32[]{:S(2)}, u32[]{:S(2)}) collective-permute-start(bf16[2,128,512]{2,1,0:T(8,128)(2,1)S(1)} %get-tuple-element.340), channel_id=1, source_target_pairs={{0,1},{1,2},{2,3},{3,7},{7,6},{6,5},{5,4},{4,0},{8,9},{9,10},{10,1... | collective-permute-start | bytes 786440 | tf_op jit(solution)/shard_map/ppermute | solution.py:454
  188.3 16.0 %collective-permute-start.70 = (bf16[128,2048]{1,0:T(8,128)(2,1)S(1)}, bf16[128,2048]{1,0:T(8,128)(2,1)S(1)}, u32[]{:S(2)}, u32[]{:S(2)}) collective-permute-start(bf16[128,2048]{1,0:T(8,128)(2,1)S(1)} %get-tuple-element.346), channel_id=1, source_target_pairs={{0,8},{4,12},{8,0},{12,4},{1,9},{5,13},{9,1},{13,5},{2,10},{6,14},... | collective-permute-start | bytes 1572872 | tf_op jit(solution)/shard_map/ppermute | solution.py:370
  (59 other events, 420.8 us)

commit v2 on v1

--- a/solution.py
+++ b/solution.py
@@ -348,8 +348,10 @@
 
 
 def pieces(group, n_unit):
-    if n_unit % 2 or group == [1]:
+    if n_unit % 2:
         return [(u, 1) for u in range(n_unit)]
+    if group == [1] and n_unit > 2:
+        return [(0, 1), (1, n_unit - 2), (n_unit - 1, 1)]
     halves = [(u, 2) for u in range(0, n_unit, 2)]
     return halves if group == [0] else halves[:-1] + [(n_unit - 2, 1), (n_unit - 1, 1)]
 
@@ -389,7 +391,7 @@
     def compute(group, u):
         def run(tok):
             hand_on = group == [0] and u == min(1, n_unit - 1)
-            pa, pb, *passed, tok = partials(tok, [xs[d] for d in group], gate, up, gm, um, u, units, hand_on, group != [0])
+            pa, pb, *passed, tok = partials(tok, [xs[d] for d in group], gate, up, gm, um, u, units, hand_on, group != [0] or u > 1)
             if hand_on:
                 for d in [*range(2, n_row), 1]:
                     xs[d] = swap(passed[0], d)

time: 208 us -> 207 us (level)
  waiting for transfers between devices: 20 us -> 24 us
  Pallas kernels: 104 us -> 101 us
    ppermute x18, waiting for transfers between devices: 2.6 us -> 4.94 us  [shards(): left_came[t] = lax.ppermute(left_on[t], ('row', 'col'), to_left)]
    pallas_call x9 -> x8, Pallas kernels: 41 us -> 38.8 us  [project(): pl.pallas_call(functools.partial(project_kernel, tuple((h[:3] for h in hi...]
  transfers between devices with their start and end apart: 78 -> 78, of which waited for: 18 -> 18; matrix products, arithmetic and copies ran while one was open for 0% -> 0% of each run, Pallas kernels for 48% -> 47%
where the time goes in v2:
time: 207 us
  Pallas kernels  101 us (49%)
  starting transfers between devices  76.3 us (37%)
  waiting for transfers between devices  24 us (12%)
  local copies, waits for them, and re-layouts  3.5 us (2%)
    pallas_call x12, Pallas kernels, partials(): pl.pallas_call(functools.partial(partial_kernel, depth // gm.shape[0], un...  52.1 us
    pallas_call x8, Pallas kernels, project(): pl.pallas_call(functools.partial(project_kernel, tuple((h[:3] for h in hi...  38.8 us
    ppermute x18, starting transfers between devices, shards(): right_got[t] = lax.ppermute(sums[1], ('row', 'col'), to_right)  34.2 us
    ppermute x18, starting transfers between devices, shards(): right_came[t] = lax.ppermute(right_on[t], ('row', 'col'), to_right)  31.5 us
    ppermute x18, waiting for transfers between devices, shards(): left_got[t] = lax.ppermute(sums[0], ('row', 'col'), to_left)  15 us
    pallas_call x18, Pallas kernels, sum_step(): pl.pallas_call(functools.partial(sum_kernel, own, n_col, goes_on, ends),...  7.61 us
    ppermute x18, starting transfers between devices, shards(): left_got[t] = lax.ppermute(sums[0], ('row', 'col'), to_left)  6.44 us
    ppermute x18, waiting for transfers between devices, shards(): left_came[t] = lax.ppermute(left_on[t], ('row', 'col'), to_left)  4.94 us
  transfers between devices with their start and end apart: 78, of which 18 were waited for; matrix products, arithmetic and copies ran while one was open for 0% of the time, Pallas kernels for 47%

profile of v2, /device:TPU:0, one launch (start us, length us, event | category | flops | bytes accessed | tf_op | source)
XLA Modules:
  0.0 206.7 jit_solution(11352168579919080591)
XLA Ops:
  2.4 4.5 %shard_map.73 = (bf16[2,128,512]{2,1,0:T(8,128)(2,1)S(1)}, bf16[2,128,512]{2,1,0:T(8,128)(2,1)S(1)}, f32[8,128]{1,0:T(8,128)S(1)}) custom-call(s32[16,32]{1,0:T(8,128)S(1)} %copy-done.4, s32[16,32]{1,0:T(8,128)S(1)} %copy-done.6, bf16[2048,4096]{1,0:T(8,128)(2,1)} %gate.23, bf16[2048,4096]{1,0:T(8,128)(2,1)} %up.23, bf16[128,2048]{1,0:T(8,128)(2,1)S(1)} %copy-done), custom_call_target="tpu_custom_call" | custom-call | flops 6442450944 | bytes 16777216 | tf_op jit(solution)/shard_map/pallas_call | solution.py:89
  7.4 2.6 %collective-permute-start.1 = (bf16[2,128,512]{2,1,0:T(8,128)(2,1)S(1)}, bf16[2,128,512]{2,1,0:T(8,128)(2,1)S(1)}, u32[]{:S(2)}, u32[]{:S(2)}) collective-permute-start(bf16[2,128,512]{2,1,0:T(8,128)(2,1)S(1)} %get-tuple-element.185.rest_3_.rest_5_.rest_7_), channel_id=1, source_target_pairs={{0,1},{1,2},{2,3},{3,7},{7,6},{6,5},{5,4},{4,0},{8,9},{9,10},{10,1... | collective-permute-start | bytes 786440 | tf_op jit(solution)/shard_map/ppermute | solution.py:456
  10.0 5.1 %shard_map.74 = (bf16[2,128,512]{2,1,0:T(8,128)(2,1)S(1)}, bf16[2,128,512]{2,1,0:T(8,128)(2,1)S(1)}, bf16[128,2048]{1,0:T(8,128)(2,1)}, f32[8,128]{1,0:T(8,128)S(1)}) custom-call(s32[16,32]{1,0:T(8,128)S(1)} %copy-done.4, s32[16,32]{1,0:T(8,128)S(1)} %copy-done.6, bf16[2048,4096]{1,0:T(8,128)(2,1)} %gate.23, ...), custom_call_target="tpu_custom_call", output_to_operand_aliasing={{3}: (4, {})} | custom-call | flops 6442450944 | bytes 16777216 | tf_op jit(solution)/shard_map/pallas_call | solution.py:89
  19.3 4.0 %shard_map.76 = (bf16[2,128,512]{2,1,0:T(8,128)(2,1)S(1)}, bf16[2,128,512]{2,1,0:T(8,128)(2,1)S(1)}, f32[8,128]{1,0:T(8,128)S(1)}) custom-call(s32[16,32]{1,0:T(8,128)S(1)} %copy-done.5, s32[16,32]{1,0:T(8,128)S(1)} %copy-done.7, bf16[2048,4096]{1,0:T(8,128)(2,1)} %gate.23, bf16[2048,4096]{1,0:T(8,128)(2,1)} %up.23, ...), custom_call_target="tpu_custom_call", output_to_operand_aliasing={{2}: (4, {})} | custom-call | flops 6442450944 | bytes 16777216 | tf_op jit(solution)/shard_map/pallas_call | solution.py:89
  28.2 4.0 %shard_map.78 = (bf16[2,128,512]{2,1,0:T(8,128)(2,1)S(1)}, bf16[2,128,512]{2,1,0:T(8,128)(2,1)S(1)}, f32[8,128]{1,0:T(8,128)S(1)}) custom-call(s32[16,32]{1,0:T(8,128)S(1)} %copy-done.5, s32[16,32]{1,0:T(8,128)S(1)} %copy-done.7, bf16[2048,4096]{1,0:T(8,128)(2,1)} %gate.23, bf16[2048,4096]{1,0:T(8,128)(2,1)} %up.23, ...), custom_call_target="tpu_custom_call", output_to_operand_aliasing={{2}: (4, {})} | custom-call | flops 6442450944 | bytes 16777216 | tf_op jit(solution)/shard_map/pallas_call | solution.py:89
  39.6 4.6 %shard_map.81 = (bf16[2,256,512]{2,1,0:T(8,128)(2,1)S(1)}, bf16[2,256,512]{2,1,0:T(8,128)(2,1)S(1)}, f32[8,128]{1,0:T(8,128)S(1)}) custom-call(s32[16,32]{1,0:T(8,128)S(1)} %copy-done.5, s32[16,32]{1,0:T(8,128)S(1)} %copy-done.7, bf16[2048,4096]{1,0:T(8,128)(2,1)} %gate.23, bf16[2048,4096]{1,0:T(8,128)(2,1)} %up.23, ...), custom_call_target="tpu_custom_call", output_to_operand_aliasing={{2}: (4, {})} | custom-call | flops 6442450944 | bytes 16777216 | tf_op jit(solution)/shard_map/pallas_call | solution.py:89
  50.8 4.2 %collective-permute-done.12.left_in = bf16[2,128,512]{2,1,0:T(8,128)(2,1)} collective-permute-done((bf16[2,128,512]{2,1,0:T(8,128)(2,1)}, bf16[2,128,512]{2,1,0:T(8,128)(2,1)}, u32[]{:S(2)}, u32[]{:S(2)}) %collective-permute-start.12) | collective-permute-done | bytes 262176 | tf_op jit(solution)/shard_map/ppermute | solution.py:455
  60.8 2.0 collective-permute-start.18
  62.8 4.6 %shard_map.86 = (bf16[2,256,512]{2,1,0:T(8,128)(2,1)S(1)}, bf16[2,256,512]{2,1,0:T(8,128)(2,1)S(1)}, f32[8,128]{1,0:T(8,128)S(1)}) custom-call(s32[16,32]{1,0:T(8,128)S(1)} %copy-done.5, s32[16,32]{1,0:T(8,128)S(1)} %copy-done.7, bf16[2048,4096]{1,0:T(8,128)(2,1)} %gate.23, bf16[2048,4096]{1,0:T(8,128)(2,1)} %up.23, ...), custom_call_target="tpu_custom_call", output_to_operand_aliasing={{2}: (4, {})} | custom-call | flops 6442450944 | bytes 16777216 | tf_op jit(solution)/shard_map/pallas_call | solution.py:89
  72.0 4.6 %shard_map.89 = (bf16[2,256,512]{2,1,0:T(8,128)(2,1)S(1)}, bf16[2,256,512]{2,1,0:T(8,128)(2,1)S(1)}, f32[8,128]{1,0:T(8,128)S(1)}) custom-call(s32[16,32]{1,0:T(8,128)S(1)} %copy-done.5, s32[16,32]{1,0:T(8,128)S(1)} %copy-done.7, bf16[2048,4096]{1,0:T(8,128)(2,1)} %gate.23, bf16[2048,4096]{1,0:T(8,128)(2,1)} %up.23, ...), custom_call_target="tpu_custom_call", output_to_operand_aliasing={{2}: (4, {})} | custom-call | flops 6442450944 | bytes 16777216 | tf_op jit(solution)/shard_map/pallas_call | solution.py:89
  81.4 6.4 %shard_map.92 = (f32[128,2048]{1,0:T(8,128)S(1)}, f32[8,128]{1,0:T(8,128)S(1)}) custom-call(s32[1]{0:T(128)} %bitcast.z_ref, s32[32,16]{1,0:T(8,128)S(1)} %copy.67.mask, f32[8,128]{1,0:T(8,128)S(1)} %get-tuple-element.238.tok, bf16[4096,2048]{1,0:T(8,128)(2,1)} %down.15, bf16[128,512]{1,0:T(8,128)(2,1)S(1)} %copy-done.11, ...), custom_call_target="tpu_custom_call", output_to_operand_aliasing={{1}: (2, {})} | custom-call | flops 6442450944 | bytes 16777216 | tf_op jit(solution)/shard_map/pallas_call | solution.py:302
  88.2 2.0 collective-permute-start.29
  92.1 4.6 %shard_map.95 = (bf16[2,256,512]{2,1,0:T(8,128)(2,1)S(1)}, bf16[2,256,512]{2,1,0:T(8,128)(2,1)S(1)}, f32[8,128]{1,0:T(8,128)S(1)}) custom-call(s32[16,32]{1,0:T(8,128)S(1)} %copy-done.5, s32[16,32]{1,0:T(8,128)S(1)} %copy-done.7, bf16[2048,4096]{1,0:T(8,128)(2,1)} %gate.23, bf16[2048,4096]{1,0:T(8,128)(2,1)} %up.23, ...), custom_call_target="tpu_custom_call", output_to_operand_aliasing={{2}: (4, {})} | custom-call | flops 6442450944 | bytes 16777216 | tf_op jit(solution)/shard_map/pallas_call | solution.py:89
  97.7 2.0 collective-permute-start.33
  101.2 5.3 %shard_map.98 = (bf16[128,2048]{1,0:T(8,128)(2,1)S(1)}, f32[8,128]{1,0:T(8,128)S(1)}) custom-call(s32[1]{0:T(128)} %bitcast.z_ref, s32[32,16]{1,0:T(8,128)S(1)} %copy.67.mask, f32[8,128]{1,0:T(8,128)S(1)} %get-tuple-element.256.tok, bf16[4096,2048]{1,0:T(8,128)(2,1)} %down.15, ...), custom_call_target="tpu_custom_call", output_to_operand_aliasing={{1}: (2, {})} | custom-call | flops 6442450944 | bytes 16777216 | tf_op jit(solution)/shard_map/pallas_call | solution.py:302
  111.0 4.0 %shard_map.101 = (bf16[2,128,512]{2,1,0:T(8,128)(2,1)S(1)}, bf16[2,128,512]{2,1,0:T(8,128)(2,1)S(1)}, f32[8,128]{1,0:T(8,128)S(1)}) custom-call(s32[16,32]{1,0:T(8,128)S(1)} %copy-done.5, s32[16,32]{1,0:T(8,128)S(1)} %copy-done.7, bf16[2048,4096]{1,0:T(8,128)(2,1)} %gate.23, bf16[2048,4096]{1,0:T(8,128)(2,1)} %up.23, ...), custom_call_target="tpu_custom_call", output_to_operand_aliasing={{2}: (4, {})} | custom-call | flops 6442450944 | bytes 16777216 | tf_op jit(solution)/shard_map/pallas_call | solution.py:89
  119.5 4.0 %shard_map.104 = (bf16[2,128,512]{2,1,0:T(8,128)(2,1)S(1)}, bf16[2,128,512]{2,1,0:T(8,128)(2,1)S(1)}, f32[8,128]{1,0:T(8,128)S(1)}) custom-call(s32[16,32]{1,0:T(8,128)S(1)} %copy-done.5, s32[16,32]{1,0:T(8,128)S(1)} %copy-done.7, bf16[2048,4096]{1,0:T(8,128)(2,1)} %gate.23, bf16[2048,4096]{1,0:T(8,128)(2,1)} %up.23, ...), custom_call_target="tpu_custom_call", output_to_operand_aliasing={{2}: (4, {})} | custom-call | flops 6442450944 | bytes 16777216 | tf_op jit(solution)/shard_map/pallas_call | solution.py:89
  124.7 2.0 collective-permute-start.46
  128.7 4.0 %shard_map.107 = (bf16[2,128,512]{2,1,0:T(8,128)(2,1)S(1)}, bf16[2,128,512]{2,1,0:T(8,128)(2,1)S(1)}, f32[8,128]{1,0:T(8,128)S(1)}) custom-call(s32[16,32]{1,0:T(8,128)S(1)} %copy-done.5, s32[16,32]{1,0:T(8,128)S(1)} %copy-done.7, bf16[2048,4096]{1,0:T(8,128)(2,1)} %gate.23, bf16[2048,4096]{1,0:T(8,128)(2,1)} %up.23, ...), custom_call_target="tpu_custom_call", output_to_operand_aliasing={{2}: (4, {})} | custom-call | flops 6442450944 | bytes 16777216 | tf_op jit(solution)/shard_map/pallas_call | solution.py:89
  133.4 2.0 collective-permute-start.50
  137.2 6.1 %shard_map.110 = (f32[256,2048]{1,0:T(8,128)S(1)}, f32[8,128]{1,0:T(8,128)S(1)}) custom-call(s32[1]{0:T(128)} %bitcast.z_ref, s32[32,16]{1,0:T(8,128)S(1)} %copy.67.mask, f32[8,128]{1,0:T(8,128)S(1)} %get-tuple-element.296.tok, bf16[4096,2048]{1,0:T(8,128)(2,1)} %down.15, ...), custom_call_target="tpu_custom_call", output_to_operand_aliasing={{1}: (2, {})} | custom-call | flops 6442450944 | bytes 16777216 | tf_op jit(solution)/shard_map/pallas_call | solution.py:302
  147.8 4.0 %shard_map.113 = (bf16[2,128,512]{2,1,0:T(8,128)(2,1)S(1)}, bf16[2,128,512]{2,1,0:T(8,128)(2,1)S(1)}, f32[8,128]{1,0:T(8,128)S(1)}) custom-call(s32[16,32]{1,0:T(8,128)S(1)} %copy-done.5, s32[16,32]{1,0:T(8,128)S(1)} %copy-done.7, bf16[2048,4096]{1,0:T(8,128)(2,1)} %gate.23, bf16[2048,4096]{1,0:T(8,128)(2,1)} %up.23, ...), custom_call_target="tpu_custom_call", output_to_operand_aliasing={{2}: (4, {})} | custom-call | flops 6442450944 | bytes 16777216 | tf_op jit(solution)/shard_map/pallas_call | solution.py:89
  152.5 2.0 collective-permute-start.58
  156.3 4.3 %shard_map.116 = (f32[256,2048]{1,0:T(8,128)S(1)}, f32[8,128]{1,0:T(8,128)S(1)}) custom-call(s32[1]{0:T(128)} %bitcast.z_ref, s32[32,16]{1,0:T(8,128)S(1)} %copy.67.mask, f32[8,128]{1,0:T(8,128)S(1)} %get-tuple-element.316.tok, bf16[4096,2048]{1,0:T(8,128)(2,1)} %down.15, ...), custom_call_target="tpu_custom_call", output_to_operand_aliasing={{1}: (2, {}), {0}: (20, {})} | custom-call | flops 6442450944 | bytes 16777216 | tf_op jit(solution)/shard_map/pallas_call | solution.py:302
  165.0 4.4 %collective-permute-done.61.left_in = bf16[2,128,512]{2,1,0:T(8,128)(2,1)S(1)} collective-permute-done((bf16[2,128,512]{2,1,0:T(8,128)(2,1)S(1)}, bf16[2,128,512]{2,1,0:T(8,128)(2,1)S(1)}, u32[]{:S(2)}, u32[]{:S(2)}) %collective-permute-start.61) | collective-permute-done | bytes 262176 | tf_op jit(solution)/shard_map/ppermute | solution.py:455
  169.9 2.4 %collective-permute-start.66 = (bf16[2,128,512]{2,1,0:T(8,128)(2,1)S(1)}, bf16[2,128,512]{2,1,0:T(8,128)(2,1)S(1)}, u32[]{:S(2)}, u32[]{:S(2)}) collective-permute-start(bf16[2,128,512]{2,1,0:T(8,128)(2,1)S(1)} %get-tuple-element.338), channel_id=1, source_target_pairs={{0,1},{1,2},{2,3},{3,7},{7,6},{6,5},{5,4},{4,0},{8,9},{9,10},{10,1... | collective-permute-start | bytes 786440 | tf_op jit(solution)/shard_map/ppermute | solution.py:456
  172.4 2.5 %collective-permute-start.67 = (bf16[128,512]{1,0:T(8,128)(2,1)S(1)}, bf16[128,512]{1,0:T(8,128)(2,1)S(1)}, u32[]{:S(2)}, u32[]{:S(2)}) collective-permute-start(bf16[128,512]{1,0:T(8,128)(2,1)S(1)} %get-tuple-element.333.rest_14_.rest_4_.rest_2_.rest_8_), channel_id=1, source_target_pairs={{0,1},{1,2},{2,3},{3,7},{7,6},{6,5},{5,4},{4,0},{8,9},{9,10},{10,1... | collective-permute-start | bytes 393224 | tf_op jit(solution)/shard_map/ppermute | solution.py:461
  174.9 4.3 %shard_map.121 = (bf16[128,2048]{1,0:T(8,128)(2,1)S(1)}, bf16[128,2048]{1,0:T(8,128)(2,1)S(1)}, f32[8,128]{1,0:T(8,128)S(1)}) custom-call(s32[1]{0:T(128)} %bitcast.z_ref, s32[32,16]{1,0:T(8,128)S(1)} %copy.67.mask, f32[8,128]{1,0:T(8,128)S(1)} %get-tuple-element.332.tok, bf16[4096,2048]{1,0:T(8,128)(2,1)} %down.15, ...), custom_call_target="tpu_custom_call", output_to_operand_aliasing={{2}: (2, {})} | custom-call | flops 6442450944 | bytes 16777216 | tf_op jit(solution)/shard_map/pallas_call | solution.py:302
  181.6 3.8 %shard_map.125 = (f32[128,2048]{1,0:T(8,128)S(1)}, f32[8,128]{1,0:T(8,128)S(1)}) custom-call(s32[1]{0:T(128)} %bitcast.z_ref, s32[32,16]{1,0:T(8,128)S(1)} %copy.67.mask, f32[8,128]{1,0:T(8,128)S(1)} %get-tuple-element.345.tok, bf16[4096,2048]{1,0:T(8,128)(2,1)} %down.15, ...), custom_call_target="tpu_custom_call", output_to_operand_aliasing={{1}: (2, {})} | custom-call | flops 6442450944 | bytes 16777216 | tf_op jit(solution)/shard_map/pallas_call | solution.py:302
  190.8 3.5 %collective-permute-done.74.rest_1_ = bf16[128,512]{1,0:T(8,128)(2,1)S(1)} collective-permute-done((bf16[128,512]{1,0:T(8,128)(2,1)S(1)}, bf16[128,512]{1,0:T(8,128)(2,1)S(1)}, u32[]{:S(2)}, u32[]{:S(2)}) %collective-permute-start.74) | collective-permute-done | bytes 131104 | tf_op jit(solution)/shard_map/ppermute | solution.py:460
  194.9 5.3 %shard_map.128 = (f32[128,2048]{1,0:T(8,128)S(1)}, f32[8,128]{1,0:T(8,128)S(1)}) custom-call(s32[1]{0:T(128)} %bitcast.z_ref, s32[32,16]{1,0:T(8,128)S(1)} %copy.67.mask, f32[8,128]{1,0:T(8,128)S(1)} %get-tuple-element.352.tok, bf16[4096,2048]{1,0:T(8,128)(2,1)} %down.15, ...), custom_call_target="tpu_custom_call", output_to_operand_aliasing={{1}: (2, {}), {0}: (20, {})} | custom-call | flops 6442450944 | bytes 16777216 | tf_op jit(solution)/shard_map/pallas_call | solution.py:302
  200.2 3.5 %shard_map.129 = (bf16[128,2048]{1,0:T(8,128)(2,1)S(1)}, f32[8,128]{1,0:T(8,128)S(1)}) custom-call(s32[1]{0:T(128)} %bitcast.z_ref, s32[32,16]{1,0:T(8,128)S(1)} %copy.67.mask, f32[8,128]{1,0:T(8,128)S(1)} %get-tuple-element.356.tok, bf16[4096,2048]{1,0:T(8,128)(2,1)} %down.15, ...), custom_call_target="tpu_custom_call", output_to_operand_aliasing={{1}: (2, {})} | custom-call | flops 6442450944 | bytes 16777216 | tf_op jit(solution)/shard_map/pallas_call | solution.py:302
  (209 shorter events, 83.3 us)
Async XLA Ops:
  6.9 10.2 %collective-permute-start = (bf16[2,128,512]{2,1,0:T(8,128)(2,1)S(1)}, bf16[2,128,512]{2,1,0:T(8,128)(2,1)S(1)}, u32[]{:S(2)}, u32[]{:S(2)}) collective-permute-start(bf16[2,128,512]{2,1,0:T(8,128)(2,1)S(1)} %get-tuple-element.184.rest_0_), channel_id=1, source_target_pairs={{1,0},{2,1},{3,2},{7,3},{6,7},{5,6},{4,5},{0,4},{9,8},{10,9},{11,1... | collective-permute-start | bytes 786440 | tf_op jit(solution)/shard_map/ppermute | solution.py:455
  7.4 9.8 %collective-permute-start.1 = (bf16[2,128,512]{2,1,0:T(8,128)(2,1)S(1)}, bf16[2,128,512]{2,1,0:T(8,128)(2,1)S(1)}, u32[]{:S(2)}, u32[]{:S(2)}) collective-permute-start(bf16[2,128,512]{2,1,0:T(8,128)(2,1)S(1)} %get-tuple-element.185.rest_3_.rest_5_.rest_7_), channel_id=1, source_target_pairs={{0,1},{1,2},{2,3},{3,7},{7,6},{6,5},{5,4},{4,0},{8,9},{9,10},{10,1... | collective-permute-start | bytes 786440 | tf_op jit(solution)/shard_map/ppermute | solution.py:456
  15.1 24.5 %collective-permute-start.6 = (bf16[128,2048]{1,0:T(8,128)(2,1)}, bf16[128,2048]{1,0:T(8,128)(2,1)S(1)}, u32[]{:S(2)}, u32[]{:S(2)}) collective-permute-start(bf16[128,2048]{1,0:T(8,128)(2,1)} %get-tuple-element.203), channel_id=1, source_target_pairs={{8,0},{12,4},{0,8},{4,12},{9,1},{13,5},{1,9},{5,13},{10,2},{14,6},... | collective-permute-start | bytes 1572872 | tf_op jit(solution)/shard_map/ppermute | solution.py:372
  17.1 22.5 %collective-permute-start.7 = (bf16[128,2048]{1,0:T(8,128)(2,1)}, bf16[128,2048]{1,0:T(8,128)(2,1)S(1)}, u32[]{:S(2)}, u32[]{:S(2)}) collective-permute-start(bf16[128,2048]{1,0:T(8,128)(2,1)} %get-tuple-element.203), channel_id=1, source_target_pairs={{12,0},{8,4},{4,8},{0,12},{13,1},{9,5},{5,9},{1,13},{14,2},{10,6},... | collective-permute-start | bytes 1572872 | tf_op jit(solution)/shard_map/ppermute | solution.py:372
  35.0 9.3 %collective-permute-start.8 = (bf16[2,128,512]{2,1,0:T(8,128)(2,1)S(1)}, bf16[2,128,512]{2,1,0:T(8,128)(2,1)S(1)}, u32[]{:S(2)}, u32[]{:S(2)}) collective-permute-start(bf16[2,128,512]{2,1,0:T(8,128)(2,1)S(1)} %get-tuple-element.205), channel_id=1, source_target_pairs={{1,0},{2,1},{3,2},{7,3},{6,7},{5,6},{4,5},{0,4},{9,8},{10,9},{11,1... | collective-permute-start | bytes 786440 | tf_op jit(solution)/shard_map/ppermute | solution.py:455
  37.7 10.3 %collective-permute-start.10 = (bf16[128,512]{1,0:T(8,128)(2,1)S(1)}, bf16[128,512]{1,0:T(8,128)(2,1)S(1)}, u32[]{:S(2)}, u32[]{:S(2)}) collective-permute-start(bf16[128,512]{1,0:T(8,128)(2,1)S(1)} %get-tuple-element.211.rest_0_), channel_id=1, source_target_pairs={{0,1},{1,2},{2,3},{3,7},{7,6},{6,5},{5,4},{4,0},{8,9},{9,10},{10,1... | collective-permute-start | bytes 393224 | tf_op jit(solution)/shard_map/ppermute | solution.py:461
  45.5 9.5 %collective-permute-start.12 = (bf16[2,128,512]{2,1,0:T(8,128)(2,1)}, bf16[2,128,512]{2,1,0:T(8,128)(2,1)}, u32[]{:S(2)}, u32[]{:S(2)}) collective-permute-start(bf16[2,128,512]{2,1,0:T(8,128)(2,1)} %get-tuple-element.214), channel_id=1, source_target_pairs={{1,0},{2,1},{3,2},{7,3},{6,7},{5,6},{4,5},{0,4},{9,8},{10,9},{11,1... | collective-permute-start | bytes 786440 | tf_op jit(solution)/shard_map/ppermute | solution.py:455
  48.7 11.1 %collective-permute-start.14 = (bf16[128,512]{1,0:T(8,128)(2,1)}, bf16[128,512]{1,0:T(8,128)(2,1)}, u32[]{:S(2)}, u32[]{:S(2)}) collective-permute-start(bf16[128,512]{1,0:T(8,128)(2,1)} %get-tuple-element.218.rest_2_.rest_8_), channel_id=1, source_target_pairs={{0,1},{1,2},{2,3},{3,7},{7,6},{6,5},{5,4},{4,0},{8,9},{9,10},{10,1... | collective-permute-start | bytes 393224 | tf_op jit(solution)/shard_map/ppermute | solution.py:461
  50.7 9.1 %collective-permute-start.15 = (bf16[128,512]{1,0:T(8,128)(2,1)}, bf16[128,512]{1,0:T(8,128)(2,1)}, u32[]{:S(2)}, u32[]{:S(2)}) collective-permute-start(bf16[128,512]{1,0:T(8,128)(2,1)} %get-tuple-element.219.rest_3_.rest_9_), channel_id=1, source_target_pairs={{1,0},{2,1},{3,2},{7,3},{6,7},{5,6},{4,5},{0,4},{9,8},{10,9},{11,1... | collective-permute-start | bytes 393224 | tf_op jit(solution)/shard_map/ppermute | solution.py:460
  50.7 60.3 %collective-permute-start.36 = (bf16[128,2048]{1,0:T(8,128)(2,1)}, bf16[128,2048]{1,0:T(8,128)(2,1)S(1)}, u32[]{:S(2)}, u32[]{:S(2)}) collective-permute-start(bf16[128,2048]{1,0:T(8,128)(2,1)} %get-tuple-element.203), channel_id=1, source_target_pairs={{4,0},{0,4},{12,8},{8,12},{5,1},{1,5},{13,9},{9,13},{6,2},{2,6},{1... | collective-permute-start | bytes 1572872 | tf_op jit(solution)/shard_map/ppermute | solution.py:372
  57.3 10.1 %collective-permute-start.16 = (bf16[2,128,512]{2,1,0:T(8,128)(2,1)S(1)}, bf16[2,128,512]{2,1,0:T(8,128)(2,1)S(1)}, u32[]{:S(2)}, u32[]{:S(2)}) collective-permute-start(bf16[2,128,512]{2,1,0:T(8,128)(2,1)S(1)} %get-tuple-element.222), channel_id=1, source_target_pairs={{1,0},{2,1},{3,2},{7,3},{6,7},{5,6},{4,5},{0,4},{9,8},{10,9},{11,1... | collective-permute-start | bytes 786440 | tf_op jit(solution)/shard_map/ppermute | solution.py:455
  58.3 9.1 %collective-permute-start.17 = (bf16[2,128,512]{2,1,0:T(8,128)(2,1)S(1)}, bf16[2,128,512]{2,1,0:T(8,128)(2,1)S(1)}, u32[]{:S(2)}, u32[]{:S(2)}) collective-permute-start(bf16[2,128,512]{2,1,0:T(8,128)(2,1)S(1)} %get-tuple-element.223), channel_id=1, source_target_pairs={{0,1},{1,2},{2,3},{3,7},{7,6},{6,5},{5,4},{4,0},{8,9},{9,10},{10,1... | collective-permute-start | bytes 786440 | tf_op jit(solution)/shard_map/ppermute | solution.py:456
  60.8 9.0 %collective-permute-start.18 = (bf16[128,512]{1,0:T(8,128)(2,1)S(1)}, bf16[128,512]{1,0:T(8,128)(2,1)S(1)}, u32[]{:S(2)}, u32[]{:S(2)}) collective-permute-start(bf16[128,512]{1,0:T(8,128)(2,1)S(1)} %get-tuple-element.228.rest_4_.rest_10_.rest_0_), channel_id=1, source_target_pairs={{0,1},{1,2},{2,3},{3,7},{7,6},{6,5},{5,4},{4,0},{8,9},{9,10},{10,1... | collective-permute-start | bytes 393224 | tf_op jit(solution)/shard_map/ppermute | solution.py:461
  70.0 9.3 %collective-permute-start.22 = (bf16[128,512]{1,0:T(8,128)(2,1)S(1)}, bf16[128,512]{1,0:T(8,128)(2,1)S(1)}, u32[]{:S(2)}, u32[]{:S(2)}) collective-permute-start(bf16[128,512]{1,0:T(8,128)(2,1)S(1)} %get-tuple-element.236.rest_6_.rest_12_.rest_2_.rest_8_), channel_id=1, source_target_pairs={{0,1},{1,2},{2,3},{3,7},{7,6},{6,5},{5,4},{4,0},{8,9},{9,10},{10,1... | collective-permute-start | bytes 393224 | tf_op jit(solution)/shard_map/ppermute | solution.py:461
  77.0 10.8 %collective-permute-start.24 = (bf16[2,128,512]{2,1,0:T(8,128)(2,1)S(1)}, bf16[2,128,512]{2,1,0:T(8,128)(2,1)S(1)}, u32[]{:S(2)}, u32[]{:S(2)}) collective-permute-start(bf16[2,128,512]{2,1,0:T(8,128)(2,1)S(1)} %get-tuple-element.242), channel_id=1, source_target_pairs={{1,0},{2,1},{3,2},{7,3},{6,7},{5,6},{4,5},{0,4},{9,8},{10,9},{11,1... | collective-permute-start | bytes 786440 | tf_op jit(solution)/shard_map/ppermute | solution.py:455
  78.1 9.7 %collective-permute-start.25 = (bf16[2,128,512]{2,1,0:T(8,128)(2,1)S(1)}, bf16[2,128,512]{2,1,0:T(8,128)(2,1)S(1)}, u32[]{:S(2)}, u32[]{:S(2)}) collective-permute-start(bf16[2,128,512]{2,1,0:T(8,128)(2,1)S(1)} %get-tuple-element.243), channel_id=1, source_target_pairs={{0,1},{1,2},{2,3},{3,7},{7,6},{6,5},{5,4},{4,0},{8,9},{9,10},{10,1... | collective-permute-start | bytes 786440 | tf_op jit(solution)/shard_map/ppermute | solution.py:456
  79.4 10.8 %collective-permute-start.26 = (bf16[128,512]{1,0:T(8,128)(2,1)S(1)}, bf16[128,512]{1,0:T(8,128)(2,1)S(1)}, u32[]{:S(2)}, u32[]{:S(2)}) collective-permute-start(bf16[128,512]{1,0:T(8,128)(2,1)S(1)} %get-tuple-element.239.rest_14_.rest_4_.rest_10_.rest_0_), channel_id=1, source_target_pairs={{0,1},{1,2},{2,3},{3,7},{7,6},{6,5},{5,4},{4,0},{8,9},{9,10},{10,1... | collective-permute-start | bytes 393224 | tf_op jit(solution)/shard_map/ppermute | solution.py:461
  88.2 9.1 %collective-permute-start.28 = (bf16[2,128,512]{2,1,0:T(8,128)(2,1)S(1)}, bf16[2,128,512]{2,1,0:T(8,128)(2,1)S(1)}, u32[]{:S(2)}, u32[]{:S(2)}) collective-permute-start(bf16[2,128,512]{2,1,0:T(8,128)(2,1)S(1)} %get-tuple-element.250), channel_id=1, source_target_pairs={{1,0},{2,1},{3,2},{7,3},{6,7},{5,6},{4,5},{0,4},{9,8},{10,9},{11,1... | collective-permute-start | bytes 786440 | tf_op jit(solution)/shard_map/ppermute | solution.py:455
  88.2 9.1 %collective-permute-start.29 = (bf16[2,128,512]{2,1,0:T(8,128)(2,1)S(1)}, bf16[2,128,512]{2,1,0:T(8,128)(2,1)S(1)}, u32[]{:S(2)}, u32[]{:S(2)}) collective-permute-start(bf16[2,128,512]{2,1,0:T(8,128)(2,1)S(1)} %get-tuple-element.251), channel_id=1, source_target_pairs={{0,1},{1,2},{2,3},{3,7},{7,6},{6,5},{5,4},{4,0},{8,9},{9,10},{10,1... | collective-permute-start | bytes 786440 | tf_op jit(solution)/shard_map/ppermute | solution.py:456
  90.3 9.5 %collective-permute-start.30 = (bf16[128,512]{1,0:T(8,128)(2,1)S(1)}, bf16[128,512]{1,0:T(8,128)(2,1)S(1)}, u32[]{:S(2)}, u32[]{:S(2)}) collective-permute-start(bf16[128,512]{1,0:T(8,128)(2,1)S(1)} %get-tuple-element.254.rest_6_.rest_12_.rest_2_.rest_16_), channel_id=1, source_target_pairs={{0,1},{1,2},{2,3},{3,7},{7,6},{6,5},{5,4},{4,0},{8,9},{9,10},{10,1... | collective-permute-start | bytes 393224 | tf_op jit(solution)/shard_map/ppermute | solution.py:461
  97.7 8.9 %collective-permute-start.32 = (bf16[2,128,512]{2,1,0:T(8,128)(2,1)S(1)}, bf16[2,128,512]{2,1,0:T(8,128)(2,1)S(1)}, u32[]{:S(2)}, u32[]{:S(2)}) collective-permute-start(bf16[2,128,512]{2,1,0:T(8,128)(2,1)S(1)} %get-tuple-element.262), channel_id=1, source_target_pairs={{1,0},{2,1},{3,2},{7,3},{6,7},{5,6},{4,5},{0,4},{9,8},{10,9},{11,1... | collective-permute-start | bytes 786440 | tf_op jit(solution)/shard_map/ppermute | solution.py:455
  99.8 9.1 %collective-permute-start.34 = (bf16[128,512]{1,0:T(8,128)(2,1)S(1)}, bf16[128,512]{1,0:T(8,128)(2,1)S(1)}, u32[]{:S(2)}, u32[]{:S(2)}) collective-permute-start(bf16[128,512]{1,0:T(8,128)(2,1)S(1)} %get-tuple-element.257.rest_14_.rest_4_.rest_8_.rest_18_), channel_id=1, source_target_pairs={{0,1},{1,2},{2,3},{3,7},{7,6},{6,5},{5,4},{4,0},{8,9},{9,10},{10,1... | collective-permute-start | bytes 393224 | tf_op jit(solution)/shard_map/ppermute | solution.py:461
  106.9 9.0 %collective-permute-start.37 = (bf16[2,128,512]{2,1,0:T(8,128)(2,1)S(1)}, bf16[2,128,512]{2,1,0:T(8,128)(2,1)S(1)}, u32[]{:S(2)}, u32[]{:S(2)}) collective-permute-start(bf16[2,128,512]{2,1,0:T(8,128)(2,1)S(1)} %get-tuple-element.270), channel_id=1, source_target_pairs={{1,0},{2,1},{3,2},{7,3},{6,7},{5,6},{4,5},{0,4},{9,8},{10,9},{11,1... | collective-permute-start | bytes 786440 | tf_op jit(solution)/shard_map/ppermute | solution.py:455
  106.9 9.0 %collective-permute-start.38 = (bf16[2,128,512]{2,1,0:T(8,128)(2,1)S(1)}, bf16[2,128,512]{2,1,0:T(8,128)(2,1)S(1)}, u32[]{:S(2)}, u32[]{:S(2)}) collective-permute-start(bf16[2,128,512]{2,1,0:T(8,128)(2,1)S(1)} %get-tuple-element.271), channel_id=1, source_target_pairs={{0,1},{1,2},{2,3},{3,7},{7,6},{6,5},{5,4},{4,0},{8,9},{9,10},{10,1... | collective-permute-start | bytes 786440 | tf_op jit(solution)/shard_map/ppermute | solution.py:456
  109.0 9.3 %collective-permute-start.39 = (bf16[128,512]{1,0:T(8,128)(2,1)S(1)}, bf16[128,512]{1,0:T(8,128)(2,1)S(1)}, u32[]{:S(2)}, u32[]{:S(2)}) collective-permute-start(bf16[128,512]{1,0:T(8,128)(2,1)S(1)} %get-tuple-element.274.rest_6_.rest_10_.rest_20_.rest_24_), channel_id=1, source_target_pairs={{0,1},{1,2},{2,3},{3,7},{7,6},{6,5},{5,4},{4,0},{8,9},{9,10},{10,1... | collective-permute-start | bytes 393224 | tf_op jit(solution)/shard_map/ppermute | solution.py:461
  133.4 10.0 %collective-permute-start.49 = (bf16[2,128,512]{2,1,0:T(8,128)(2,1)S(1)}, bf16[2,128,512]{2,1,0:T(8,128)(2,1)S(1)}, u32[]{:S(2)}, u32[]{:S(2)}) collective-permute-start(bf16[2,128,512]{2,1,0:T(8,128)(2,1)S(1)} %get-tuple-element.300), channel_id=1, source_target_pairs={{1,0},{2,1},{3,2},{7,3},{6,7},{5,6},{4,5},{0,4},{9,8},{10,9},{11,1... | collective-permute-start | bytes 786440 | tf_op jit(solution)/shard_map/ppermute | solution.py:455
  133.4 9.9 %collective-permute-start.50 = (bf16[2,128,512]{2,1,0:T(8,128)(2,1)S(1)}, bf16[2,128,512]{2,1,0:T(8,128)(2,1)S(1)}, u32[]{:S(2)}, u32[]{:S(2)}) collective-permute-start(bf16[2,128,512]{2,1,0:T(8,128)(2,1)S(1)} %get-tuple-element.301), channel_id=1, source_target_pairs={{0,1},{1,2},{2,3},{3,7},{7,6},{6,5},{5,4},{4,0},{8,9},{9,10},{10,1... | collective-permute-start | bytes 786440 | tf_op jit(solution)/shard_map/ppermute | solution.py:456
  135.4 10.3 %collective-permute-start.51 = (bf16[128,512]{1,0:T(8,128)(2,1)S(1)}, bf16[128,512]{1,0:T(8,128)(2,1)S(1)}, u32[]{:S(2)}, u32[]{:S(2)}) collective-permute-start(bf16[128,512]{1,0:T(8,128)(2,1)S(1)} %get-tuple-element.297.rest_30_.rest_4_.rest_10_.rest_0_), channel_id=1, source_target_pairs={{0,1},{1,2},{2,3},{3,7},{7,6},{6,5},{5,4},{4,0},{8,9},{9,10},{10,1... | collective-permute-start | bytes 393224 | tf_op jit(solution)/shard_map/ppermute | solution.py:461
  163.0 9.3 %collective-permute-start.63 = (bf16[128,512]{1,0:T(8,128)(2,1)S(1)}, bf16[128,512]{1,0:T(8,128)(2,1)S(1)}, u32[]{:S(2)}, u32[]{:S(2)}) collective-permute-start(bf16[128,512]{1,0:T(8,128)(2,1)S(1)} %get-tuple-element.330.rest_6_.rest_12_.rest_2_.rest_0_), channel_id=1, source_target_pairs={{0,1},{1,2},{2,3},{3,7},{7,6},{6,5},{5,4},{4,0},{8,9},{9,10},{10,1... | collective-permute-start | bytes 393224 | tf_op jit(solution)/shard_map/ppermute | solution.py:461
  169.8 9.4 %collective-permute-start.65 = (bf16[2,128,512]{2,1,0:T(8,128)(2,1)S(1)}, bf16[2,128,512]{2,1,0:T(8,128)(2,1)S(1)}, u32[]{:S(2)}, u32[]{:S(2)}) collective-permute-start(bf16[2,128,512]{2,1,0:T(8,128)(2,1)S(1)} %get-tuple-element.337), channel_id=1, source_target_pairs={{1,0},{2,1},{3,2},{7,3},{6,7},{5,6},{4,5},{0,4},{9,8},{10,9},{11,1... | collective-permute-start | bytes 786440 | tf_op jit(solution)/shard_map/ppermute | solution.py:455
  169.9 9.3 %collective-permute-start.66 = (bf16[2,128,512]{2,1,0:T(8,128)(2,1)S(1)}, bf16[2,128,512]{2,1,0:T(8,128)(2,1)S(1)}, u32[]{:S(2)}, u32[]{:S(2)}) collective-permute-start(bf16[2,128,512]{2,1,0:T(8,128)(2,1)S(1)} %get-tuple-element.338), channel_id=1, source_target_pairs={{0,1},{1,2},{2,3},{3,7},{7,6},{6,5},{5,4},{4,0},{8,9},{9,10},{10,1... | collective-permute-start | bytes 786440 | tf_op jit(solution)/shard_map/ppermute | solution.py:456
  188.3 15.5 %collective-permute-start.70 = (bf16[128,2048]{1,0:T(8,128)(2,1)S(1)}, bf16[128,2048]{1,0:T(8,128)(2,1)S(1)}, u32[]{:S(2)}, u32[]{:S(2)}) collective-permute-start(bf16[128,2048]{1,0:T(8,128)(2,1)S(1)} %get-tuple-element.344), channel_id=1, source_target_pairs={{0,8},{4,12},{8,0},{12,4},{1,9},{5,13},{9,1},{13,5},{2,10},{6,14},... | collective-permute-start | bytes 1572872 | tf_op jit(solution)/shard_map/ppermute | solution.py:372
  (59 other events, 419.8 us)
